TPU v7x, 256 devices: a whole 4x4x8 slice. The times are simulated.
256 devices in a mesh: dp: 8 (over x, core), seq: 32 (over z, y).
Axes of the slice: x: 4, y: 4, z: 8, core: 2. Of those that a mesh axis runs over, the one named last changes fastest.
Arguments:
- spatial_qkv: bfloat16 [8, 32, 128, 3456], P('dp', 'seq')
- lengths: int32 [8], P('dp'), may hold values from 4 to 32, as said below
- w_qkv: bfloat16 [1152, 3456], P('seq'), may hold values from -0.75 to 0.75
- cotangent: bfloat16 [8, 32, 128, 1152], P('dp', 'seq'), may hold values from -6 to 6
Outputs:
- block_out: bfloat16 [8, 32, 128, 1152], P('dp', 'seq')
- grad_qkv: bfloat16 [8, 32, 128, 3456], P('dp', 'seq')
- grad_w: bfloat16 [1152, 3456], P('seq', 'dp')
Inputs may be any that keep to these rules, and one draw needn't show every extreme that they name: `lengths`: every video has at least one live frame, and some video fills all 32 slots.
All inputs are finite; a program needn't handle non-finite values.
Results may differ from a plain program's by a relative error of at most 0.035.
The roundings to bfloat16 on the way count: a program that leaves them out, or rounds other values in their place, can miss the bound.
Values may be sent and summed in bfloat16 or wider, within the bound.
A program may use at most 128 MiB of HBM per device.

v0:
```python
import jax
import jax.numpy as jnp
from jax import lax
from jax.sharding import PartitionSpec as P

HEADS = 16


SPATIAL_LAYOUTS = ("blhe,bmhe->bhlm", "bhlm,bmhe->blhe", "bhlm,blhe->bmhe")
TEMPORAL_FORMS = ("lbhe,mbhe->bhlm", "bhlm,mbhe->lbhe", "bhlm,lbhe->mbhe")


def split_heads(array, head_count):
    return array.reshape(array.shape[:-1] + (head_count, array.shape[-1] // head_count))


def join_heads(array):
    return array.reshape(array.shape[:-2] + (array.shape[-2] * array.shape[-1],))


def attend_forward(queries, keys_in, values_in, key_live, forms, head_count):
    scale = (queries.shape[-1] // head_count) ** (-0.5)
    query_heads = split_heads(queries, head_count)
    key_heads = split_heads(keys_in, head_count)
    value_heads = split_heads(values_in, head_count)
    scores = (
        jnp.einsum(forms[0], query_heads, key_heads, preferred_element_type=jnp.float32) * scale
    )
    if key_live is not None:
        scores = jnp.where(key_live, scores, -1e30)
    peak = jnp.max(scores, axis=-1, keepdims=True)
    expo = jnp.exp(scores - peak)
    probs = expo / jnp.sum(expo, axis=-1, keepdims=True)
    probs_low = probs.astype(jnp.bfloat16)
    output = jnp.einsum(forms[1], probs_low, value_heads, preferred_element_type=jnp.float32)
    return (join_heads(output), probs, probs_low)


def attend_backward(grad_out, queries, keys_in, values_in, probs, probs_low, forms, head_count):
    scale = (queries.shape[-1] // head_count) ** (-0.5)
    grad_heads = split_heads(grad_out, head_count)
    query_heads = split_heads(queries, head_count)
    key_heads = split_heads(keys_in, head_count)
    value_heads = split_heads(values_in, head_count)
    grad_values = jnp.einsum(forms[2], probs_low, grad_heads, preferred_element_type=jnp.float32)
    grad_probs = jnp.einsum(forms[0], grad_heads, value_heads, preferred_element_type=jnp.float32)
    grad_scores = probs * (grad_probs - jnp.sum(grad_probs * probs, axis=-1, keepdims=True))
    scaled_low = (grad_scores * scale).astype(jnp.bfloat16)
    grad_queries = jnp.einsum(forms[1], scaled_low, key_heads, preferred_element_type=jnp.float32)
    grad_keys = jnp.einsum(forms[2], scaled_low, query_heads, preferred_element_type=jnp.float32)
    return jnp.concatenate(
        [join_heads(grad_queries), join_heads(grad_keys), join_heads(grad_values)], axis=-1
    )


def project_rows(rows, weight):
    return jnp.dot(rows, weight, preferred_element_type=jnp.float32)


def project_back(rows, weight):
    return lax.dot_general(
        rows, weight, (((1,), (1,)), ((), ())), preferred_element_type=jnp.float32
    )


def local(spatial_qkv, lengths, w_qkv, cotangent):
    model_width = w_qkv.shape[1] // 3
    head_count = HEADS
    frame_local = spatial_qkv.shape[1]
    patches = spatial_qkv.shape[2]
    w_full = lax.all_gather(w_qkv, "seq", axis=0, tiled=True)
    packed_tensor = spatial_qkv[0]
    spatial_queries = packed_tensor[..., :model_width]
    spatial_keys = packed_tensor[..., model_width : 2 * model_width]
    spatial_values = packed_tensor[..., 2 * model_width :]
    spatial_out, spatial_weights, spatial_reduced = attend_forward(
        spatial_queries, spatial_keys, spatial_values, None, SPATIAL_LAYOUTS, head_count
    )
    spatial_out = spatial_out.astype(jnp.bfloat16)
    projected = project_rows(spatial_out.reshape(-1, model_width), w_full).astype(jnp.bfloat16)
    projected = projected.reshape(1, frame_local, patches, 3 * model_width)
    moved, spatial_patch, grad_patch = (
        lax.all_to_all(projected, "seq", split_axis=2, concat_axis=1, tiled=True),
        lax.all_to_all(
            spatial_out.reshape(1, frame_local, patches, model_width),
            "seq",
            split_axis=2,
            concat_axis=1,
            tiled=True,
        ),
        lax.all_to_all(cotangent, "seq", split_axis=2, concat_axis=1, tiled=True),
    )
    moved = moved[0]
    spatial_patch = spatial_patch[0]
    grad_patch = grad_patch[0]
    frames_all = moved.shape[0]
    patch_local = moved.shape[1]
    key_live = (jnp.arange(frames_all) < lengths[0]).reshape(1, 1, 1, frames_all)
    tqueries = moved[..., :model_width]
    tkeys = moved[..., model_width : 2 * model_width]
    tvalues = moved[..., 2 * model_width :]
    temporal_out, temporal_probs, temporal_low = attend_forward(
        tqueries, tkeys, tvalues, key_live, TEMPORAL_FORMS, head_count
    )
    temporal_out = temporal_out.astype(jnp.bfloat16).reshape(
        1, frames_all, patch_local, model_width
    )
    temporal_frames = lax.all_to_all(temporal_out, "seq", split_axis=1, concat_axis=2, tiled=True)[
        0
    ]
    block_out = (spatial_out.astype(jnp.float32) + temporal_frames.astype(jnp.float32)).astype(
        jnp.bfloat16
    )
    grad_projected = attend_backward(
        grad_patch,
        tqueries,
        tkeys,
        tvalues,
        temporal_probs,
        temporal_low,
        TEMPORAL_FORMS,
        head_count,
    ).astype(jnp.bfloat16)
    act_rows = spatial_patch.reshape(-1, model_width)
    grad_rows = grad_projected.reshape(-1, 3 * model_width)
    grad_frames = lax.all_to_all(
        grad_projected.reshape(1, frames_all, patch_local, 3 * model_width),
        "seq",
        split_axis=1,
        concat_axis=2,
        tiled=True,
    )[0]
    back_term = project_back(grad_frames.reshape(-1, 3 * model_width), w_full).reshape(
        frame_local, patches, model_width
    )
    spatial_gradient = (cotangent[0].astype(jnp.float32) + back_term).astype(jnp.bfloat16)
    weight_part = lax.psum_scatter(
        lax.dot_general(
            act_rows, grad_rows, (((0,), (0,)), ((), ())), preferred_element_type=jnp.float32
        ).astype(jnp.bfloat16),
        "seq",
        scatter_dimension=0,
        tiled=True,
    )
    grad_w = lax.psum_scatter(weight_part, "dp", scatter_dimension=1, tiled=True).astype(
        jnp.float32
    )
    grad_w = grad_w.astype(jnp.bfloat16)
    grad_packed = attend_backward(
        spatial_gradient,
        spatial_queries,
        spatial_keys,
        spatial_values,
        spatial_weights,
        spatial_reduced,
        SPATIAL_LAYOUTS,
        head_count,
    ).astype(jnp.bfloat16)
    return (
        block_out.reshape(1, frame_local, patches, model_width),
        grad_packed.reshape(1, frame_local, patches, 3 * model_width),
        grad_w,
    )


def solution(mesh):
    in_specs = (P("dp", "seq", None, None), P("dp"), P("seq", None), P("dp", "seq", None, None))
    out_specs = (P("dp", "seq", None, None), P("dp", "seq", None, None), P("seq", "dp"))
    return jax.shard_map(local, mesh=mesh, in_specs=in_specs, out_specs=out_specs, check_vma=False)
```

profile of v0, /device:TPU:1, one launch (start us, length us, event | category | flops | bytes accessed | tf_op | source)
XLA Modules:
  0.0 535.7 jit_solution(6865152012451440707)
XLA Ops:
  13.1 12.0 %all-to-all-start.2 = ((bf16[32,2,2304]{2,1,0:T(2,128)(2,1)}), bf16[32,2,2304]{2,1,0:T(2,128)(2,1)S(1)}, u32[]{:S(2)}, u32[]{:S(2)}) async-start(bf16[32,2,2304]{2,1,0:T(2,128)(2,1)} %reshape.348), calls=%async_computation.2 | async-start | bytes 589824 | tf_op jit(solution)/shard_map/all_to_all | solution.py:91
  32.2 5.2 all-to-all-done.2
  37.4 6.4 %all-to-all-start.4 = ((bf16[32,2,2304]{2,1,0:T(2,128)(2,1)}), bf16[32,2,2304]{2,1,0:T(2,128)(2,1)S(1)}, u32[]{:S(2)}, u32[]{:S(2)}) async-start(bf16[32,2,2304]{2,1,0:T(2,128)(2,1)} %reshape.350), calls=%async_computation.4 | async-start | bytes 589824 | tf_op jit(solution)/shard_map/all_to_all | solution.py:84
  43.8 74.6 %all-gather.3.cloned.1.call-done = bf16[32,36,3456]{2,1,0:T(8,128)(2,1)} async-done(((bf16[1,36,3456]{2,1,0:T(8,128)(2,1)}), bf16[32,36,3456]{2,1,0:T(8,128)(2,1)}) %all-gather.3.cloned.1.call-update) | async-done | bytes 7962640 | tf_op jit(solution)/shard_map/all_gather | solution.py:71
  118.4 12.4 %reshape.336 = bf16[1152,3456]{1,0:T(8,128)(2,1)} reshape(bf16[32,36,3456]{2,1,0:T(8,128)(2,1)} %all-gather.3.cloned.1.call-done) | data formatting | bytes 15925248
  130.8 4.6 fusion.5
  136.8 6.0 %reduce.10 = bf16[128,3456]{1,0:T(8,128)(2,1)S(1)} reduce(bf16[128,1,1,3456]{3,2,1,0:T(2,128)(2,1)S(1)} %bitcast.111, bf16[]{:T(256)} %broadcast.64), dimensions={1,2}, to_apply=%bitcast.108.reduce_sub_computation | reduce | bytes 1769474
  144.3 5.4 all-to-all-start
  156.3 15.9 %all-to-all-done = bf16[32,2,6912]{2,1,0:T(2,128)(2,1)S(1)} async-done(((bf16[32,2,6912]{2,1,0:T(2,128)(2,1)}), bf16[32,2,6912]{2,1,0:T(2,128)(2,1)S(1)}, u32[]{:S(2)}, u32[]{:S(2)}) %all-to-all-start) | async-done | bytes 884768 | tf_op jit(solution)/shard_map/all_to_all | solution.py:83
  173.2 5.1 bitcast_reduce_fusion
  195.8 6.4 %all-to-all-start.1 = ((bf16[1,32,4,1152]{3,2,0,1:T(4,128)(2,1)}), bf16[1,32,4,1152]{3,2,0,1:T(4,128)(2,1)}, u32[]{:S(2)}, u32[]{:S(2)}) async-start(bf16[1,32,4,1152]{3,2,0,1:T(4,128)(2,1)} %reshape.337), calls=%async_computation.1 | async-start | bytes 589824 | tf_op jit(solution)/shard_map/all_to_all | solution.py:108
  212.1 5.4 %convolution_convert_fusion = bf16[1152,3456]{1,0:T(8,128)(2,1)} fusion(bf16[128,1152]{1,0:T(8,128)(2,1)S(1)} %concatenate.56, bf16[128,1152]{1,0:T(8,128)(2,1)S(1)} %concatenate.55, bf16[128,1152]{1,0:T(8,128)(2,1)S(1)} %concatenate.54, bf16[1,1,128,1152]{3,1,0,2:T(2,128)(2,1)S(1)} %bitcast.118), kind=kOutput, calls=%fused_computation.4 | convolution fusion | flops 1025851392 | bytes 9142272 | tf_op jit(solution)/shard_map/dot_general | solution.py:138
  217.5 9.2 %all-to-all-start.3 = ((bf16[1,32,4,3456]{3,2,0,1:T(4,128)(2,1)}), bf16[1,32,4,3456]{3,2,0,1:T(4,128)(2,1)S(1)}, u32[]{:S(2)}, u32[]{:S(2)}) async-start(bf16[1,32,4,3456]{3,2,0,1:T(4,128)(2,1)} %copy.152), calls=%async_computation.3 | async-start | bytes 1769472 | tf_op jit(solution)/shard_map/all_to_all | solution.py:126
  226.7 137.1 %fusion = bf16[48,3456]{1,0:T(8,128)(2,1)S(1)} fusion(bf16[1152,3456]{1,0:T(8,128)(2,1)} %convolution_convert_fusion), kind=kCustom, calls=%all-reduce-scatter | all-reduce-scatter fusion | flops 5308417 | bytes 8295424
  365.2 3.3 collective-permute-start.5
  368.5 4.7 collective-permute-start.7
  373.2 3.6 collective-permute-start.4
  379.5 4.1 collective-permute-done.7
  386.8 21.9 %collective-permute-start.1 = (bf16[48,3456]{1,0:T(8,128)(2,1)S(1)}, bf16[48,3456]{1,0:T(8,128)(2,1)}, u32[]{:S(2)}, u32[]{:S(2)}) collective-permute-start(bf16[48,3456]{1,0:T(8,128)(2,1)S(1)} %fusion), channel_id=1, source_target_pairs={{0,2},{1,3},{2,4},{3,5},{4,6},{5,7},{6,8},{7,9},{8,10},{9,11},{10,... | collective-permute-start | bytes 995336
  408.8 5.7 %collective-permute-start = (bf16[48,3456]{1,0:T(8,128)(2,1)S(1)}, bf16[48,3456]{1,0:T(8,128)(2,1)}, u32[]{:S(2)}, u32[]{:S(2)}) collective-permute-start(bf16[48,3456]{1,0:T(8,128)(2,1)S(1)} %fusion), channel_id=1, source_target_pairs={{0,1},{1,2},{2,3},{3,4},{4,5},{5,6},{6,7},{7,8},{8,9},{9,10},{10,1... | collective-permute-start | bytes 995336
  416.7 4.3 collective-permute-done
  421.0 33.3 %concatenate.58 = bf16[420,3456]{1,0:T(8,128)(2,1)} concatenate(bf16[36,3456]{1,0:T(8,128)(2,1)} %copy-done.19, bf16[48,3456]{1,0:T(8,128)(2,1)S(1)} %collective-permute-done.6, bf16[48,3456]{1,0:T(8,128)(2,1)S(1)} %collective-permute-done.5, bf16[48,3456]{1,0:T(8,128)(2,1)S(1)} %collective-permute-done.4, bf16[48,3456]{1,0:T(8,128)(2,1)} %collective-permute-done.3, ...), dimensions={0} | concatenate | bytes 5806080
  459.7 53.7 %reduce-scatter.6.cloned.1.call-done = bf16[432,36]{1,0:T(8,128)(2,1)} async-done(((bf16[3456,36]{1,0:T(8,128)(2,1)}), bf16[432,36]{1,0:T(8,128)(2,1)}) %reduce-scatter.6.cloned.1.call-update) | async-done | bytes 31120
  515.2 5.8 %fusion.6 = bf16[128,1152]{1,0:T(8,128)(2,1)S(1)} fusion(bf16[128,3456]{1,0:T(8,128)(2,1)S(1)} %reshape_squeeze.10, bf16[1152,3456]{1,0:T(8,128)(2,1)} %reshape.336, bf16[1,1,128,1152]{3,2,1,0:T(8,128)(2,1)S(1)} %copy-done.8), kind=kOutput, calls=%fused_computation.8 | convolution fusion | flops 1019658240 | bytes 9437184 | tf_op jit(solution)/shard_map/dot_general | solution.py:61
  (127 shorter events, 73.6 us)
Async XLA Ops:
  7.2 18.0 %copy-start.12 = (bf16[1,1,128,3456]{3,2,1,0:T(8,128)(2,1)S(1)}, bf16[1,1,128,3456]{3,2,1,0:T(8,128)(2,1)}, u32[]{:S(2)}) copy-start(bf16[1,1,128,3456]{3,2,1,0:T(8,128)(2,1)} %param.4) | copy-start | bytes 2654212
  7.2 111.2 %all-gather.3.cloned.1.call-start = ((), (), s32[]{:S(2)}) async-start(), calls=%async_computation.6 | async-start | bytes 9123840 | tf_op jit(solution)/shard_map/all_gather | solution.py:71
  13.1 24.2 %all-to-all-start.2 = ((bf16[32,2,2304]{2,1,0:T(2,128)(2,1)}), bf16[32,2,2304]{2,1,0:T(2,128)(2,1)S(1)}, u32[]{:S(2)}, u32[]{:S(2)}) async-start(bf16[32,2,2304]{2,1,0:T(2,128)(2,1)} %reshape.348), calls=%async_computation.2 | async-start | bytes 589824 | tf_op jit(solution)/shard_map/all_to_all | solution.py:91
  37.4 106.9 %all-to-all-start.4 = ((bf16[32,2,2304]{2,1,0:T(2,128)(2,1)}), bf16[32,2,2304]{2,1,0:T(2,128)(2,1)S(1)}, u32[]{:S(2)}, u32[]{:S(2)}) async-start(bf16[32,2,2304]{2,1,0:T(2,128)(2,1)} %reshape.350), calls=%async_computation.4 | async-start | bytes 589824 | tf_op jit(solution)/shard_map/all_to_all | solution.py:84
  144.3 6.3 %copy-start.11 = (bf16[32,2,2304]{2,1,0:T(2,128)(2,1)}, bf16[32,2,2304]{2,1,0:T(2,128)(2,1)S(1)}, u32[]{:S(2)}) copy-start(bf16[32,2,2304]{2,1,0:T(2,128)(2,1)S(1)} %all-to-all-done.4) | copy-start | bytes 884740
  144.3 28.0 %all-to-all-start = ((bf16[32,2,6912]{2,1,0:T(2,128)(2,1)}), bf16[32,2,6912]{2,1,0:T(2,128)(2,1)S(1)}, u32[]{:S(2)}, u32[]{:S(2)}) async-start(bf16[32,2,6912]{2,1,0:T(2,128)(2,1)} %reshape.346), calls=%async_computation | async-start | bytes 1769472 | tf_op jit(solution)/shard_map/all_to_all | solution.py:83
  153.2 28.5 %copy-start.3 = (bf16[32,4,16,72]{3,2,1,0:T(8,128)(2,1)}, bf16[32,4,16,72]{3,2,1,0:T(8,128)(2,1)S(1)}, u32[]{:S(2)}) copy-start(bf16[32,4,16,72]{3,2,1,0:T(8,128)(2,1)S(1)} %reshape_squeeze.9) | copy-start | bytes 884740
  181.7 3.7 copy-start.5
  195.8 21.7 %all-to-all-start.1 = ((bf16[1,32,4,1152]{3,2,0,1:T(4,128)(2,1)}), bf16[1,32,4,1152]{3,2,0,1:T(4,128)(2,1)}, u32[]{:S(2)}, u32[]{:S(2)}) async-start(bf16[1,32,4,1152]{3,2,0,1:T(4,128)(2,1)} %reshape.337), calls=%async_computation.1 | async-start | bytes 589824 | tf_op jit(solution)/shard_map/all_to_all | solution.py:108
  217.5 297.5 %all-to-all-start.3 = ((bf16[1,32,4,3456]{3,2,0,1:T(4,128)(2,1)}), bf16[1,32,4,3456]{3,2,0,1:T(4,128)(2,1)S(1)}, u32[]{:S(2)}, u32[]{:S(2)}) async-start(bf16[1,32,4,3456]{3,2,0,1:T(4,128)(2,1)} %copy.152), calls=%async_computation.3 | async-start | bytes 1769472 | tf_op jit(solution)/shard_map/all_to_all | solution.py:126
  226.6 188.8 %copy-start.20 = (u32[256]{0:T(256)S(1)}, u32[256]{0:T(256)}, u32[]{:S(2)}) copy-start(u32[256]{0:T(256)} %constant.15) | copy-start | bytes 3076
  226.6 286.7 %reduce-scatter.6.cloned.1.call-start = ((), (), s32[]{:S(2)}) async-start(), calls=%async_computation.7 | async-start | bytes 995328
  363.8 23.0 %collective-permute-start.6 = (bf16[48,3456]{1,0:T(8,128)(2,1)S(1)}, bf16[48,3456]{1,0:T(8,128)(2,1)S(1)}, u32[]{:S(2)}, u32[]{:S(2)}) collective-permute-start(bf16[48,3456]{1,0:T(8,128)(2,1)S(1)} %fusion), channel_id=1, source_target_pairs={{0,7},{1,8},{2,9},{3,10},{4,11},{5,12},{6,13},{7,14},{8,15},{9,16}... | collective-permute-start | bytes 995336
  365.2 43.6 %collective-permute-start.5 = (bf16[48,3456]{1,0:T(8,128)(2,1)S(1)}, bf16[48,3456]{1,0:T(8,128)(2,1)S(1)}, u32[]{:S(2)}, u32[]{:S(2)}) collective-permute-start(bf16[48,3456]{1,0:T(8,128)(2,1)S(1)} %fusion), channel_id=1, source_target_pairs={{0,6},{1,7},{2,8},{3,9},{4,10},{5,11},{6,12},{7,13},{8,14},{9,15},... | collective-permute-start | bytes 995336
  368.5 15.1 %collective-permute-start.7 = (bf16[36,3456]{1,0:T(8,128)(2,1)S(1)}, bf16[36,3456]{1,0:T(8,128)(2,1)S(1)}, u32[]{:S(2)}, u32[]{:S(2)}) collective-permute-start(bf16[36,3456]{1,0:T(8,128)(2,1)S(1)} %slice.30), channel_id=1, source_target_pairs={{0,8},{1,9},{2,10},{3,11},{4,12},{5,13},{6,14},{7,15},{8,16},{9,17... | collective-permute-start | bytes 746504
  373.2 43.5 %collective-permute-start.4 = (bf16[48,3456]{1,0:T(8,128)(2,1)S(1)}, bf16[48,3456]{1,0:T(8,128)(2,1)S(1)}, u32[]{:S(2)}, u32[]{:S(2)}) collective-permute-start(bf16[48,3456]{1,0:T(8,128)(2,1)S(1)} %fusion), channel_id=1, source_target_pairs={{0,5},{1,6},{2,7},{3,8},{4,9},{5,10},{6,11},{7,12},{8,13},{9,14},{... | collective-permute-start | bytes 995336
  376.8 39.9 %collective-permute-start.3 = (bf16[48,3456]{1,0:T(8,128)(2,1)S(1)}, bf16[48,3456]{1,0:T(8,128)(2,1)}, u32[]{:S(2)}, u32[]{:S(2)}) collective-permute-start(bf16[48,3456]{1,0:T(8,128)(2,1)S(1)} %fusion), channel_id=1, source_target_pairs={{0,4},{1,5},{2,6},{3,7},{4,8},{5,9},{6,10},{7,11},{8,12},{9,13},{1... | collective-permute-start | bytes 995336
  383.6 30.9 %copy-start.19 = (bf16[36,3456]{1,0:T(8,128)(2,1)}, bf16[36,3456]{1,0:T(8,128)(2,1)S(1)}, u32[]{:S(2)}) copy-start(bf16[36,3456]{1,0:T(8,128)(2,1)S(1)} %collective-permute-done.7) | copy-start | bytes 746500
  383.6 33.1 %collective-permute-start.2 = (bf16[48,3456]{1,0:T(8,128)(2,1)S(1)}, bf16[48,3456]{1,0:T(8,128)(2,1)}, u32[]{:S(2)}, u32[]{:S(2)}) collective-permute-start(bf16[48,3456]{1,0:T(8,128)(2,1)S(1)} %fusion), channel_id=1, source_target_pairs={{0,3},{1,4},{2,5},{3,6},{4,7},{5,8},{6,9},{7,10},{8,11},{9,12},{10... | collective-permute-start | bytes 995336
  386.8 29.9 %collective-permute-start.1 = (bf16[48,3456]{1,0:T(8,128)(2,1)S(1)}, bf16[48,3456]{1,0:T(8,128)(2,1)}, u32[]{:S(2)}, u32[]{:S(2)}) collective-permute-start(bf16[48,3456]{1,0:T(8,128)(2,1)S(1)} %fusion), channel_id=1, source_target_pairs={{0,2},{1,3},{2,4},{3,5},{4,6},{5,7},{6,8},{7,9},{8,10},{9,11},{10,... | collective-permute-start | bytes 995336
  408.8 12.2 %collective-permute-start = (bf16[48,3456]{1,0:T(8,128)(2,1)S(1)}, bf16[48,3456]{1,0:T(8,128)(2,1)}, u32[]{:S(2)}, u32[]{:S(2)}) collective-permute-start(bf16[48,3456]{1,0:T(8,128)(2,1)S(1)} %fusion), channel_id=1, source_target_pairs={{0,1},{1,2},{2,3},{3,4},{4,5},{5,6},{6,7},{7,8},{8,9},{9,10},{10,1... | collective-permute-start | bytes 995336
  459.0 56.3 %copy-start.8 = (bf16[1,1,128,1152]{3,2,1,0:T(8,128)(2,1)S(1)}, bf16[1,1,128,1152]{3,2,1,0:T(8,128)(2,1)}, u32[]{:S(2)}) copy-start(bf16[1,1,128,1152]{3,2,1,0:T(8,128)(2,1)} %param.7) | copy-start | bytes 884740
  515.2 6.1 %copy-start.16 = (bf16[1,128,1152]{1,2,0:T(8,128)(2,1)S(1)}, bf16[1,128,1152]{1,2,0:T(8,128)(2,1)}, u32[]{:S(2)}) copy-start(bf16[1,128,1152]{1,2,0:T(8,128)(2,1)} %copy-done.15) | copy-start | bytes 884740
  515.2 6.0 %copy-start.18 = (bf16[1,128,1152]{1,2,0:T(8,128)(2,1)S(1)}, bf16[1,128,1152]{1,2,0:T(8,128)(2,1)}, u32[]{:S(2)}) copy-start(bf16[1,128,1152]{1,2,0:T(8,128)(2,1)} %copy-done.17) | copy-start | bytes 884740
  (13 other events, 28.5 us)
Sparse Core Ops, SparseCore 0:
  10.6 107.7 all-gather.2
  456.7 56.6 reduce-scatter.5
where the time goes:
time: 547 us; the launch traced here: 536 us
  waiting for transfers between devices  158 us (29%)
  blocking collectives  137 us (25%)
  local copies, waits for them, and re-layouts  89 us (16%)
  starting transfers between devices  85.9 us (16%)
  matrix products  35.5 us (6%)
  between operations  16.1 us (3%)
  other arithmetic  13.6 us (2%)
    unnamed x1, blocking collectives  137 us
    all_gather x1, waiting for transfers between devices, local(): w_full = lax.all_gather(w_qkv, 'seq', axis=0, tiled=True)  74.6 us
    unnamed x11, waiting for transfers between devices  62.7 us
    unnamed x60, local copies, waits for them, and re-layouts  60.8 us
    unnamed x9, starting transfers between devices  46.5 us
    all_to_all x1, waiting for transfers between devices, local(): lax.all_to_all(projected, 'seq', split_axis=2, concat_axis=1, tiled=True)  15.9 us
    all_to_all x1, starting transfers between devices, local(): lax.all_to_all(cotangent, 'seq', split_axis=2, concat_axis=1, tiled=True)  12 us
  transfers between devices with their start and end apart: 15, of which 6 were waited for; matrix products, arithmetic and copies ran while one was open for 44% of the time, Pallas kernels for 0%

commit v1 on v0

v1 whole, which is shorter than its diff:
```python
import jax
import jax.numpy as jnp
from jax import lax
from jax.experimental import pallas as pl
from jax.experimental.pallas import tpu as pltpu
from jax.sharding import PartitionSpec as P

HEADS = 16
WIDTH = 1152
HEAD = 72
NY, NZ, NX, NC = 4, 8, 4, 2
MESH = pl.DeviceIdType.MESH
F32, BF16 = jnp.float32, jnp.bfloat16
SCALE = HEAD ** (-0.5)


def dot(a, b):
    return lax.dot_general(a, b, (((1,), (0,)), ((), ())), preferred_element_type=F32)


def dot_nt(a, b):
    return lax.dot_general(a, b, (((1,), (1,)), ((), ())), preferred_element_type=F32)


def dot_tn(a, b):
    return lax.dot_general(a, b, (((0,), (0,)), ((), ())), preferred_element_type=F32)


def half(window, j):
    return window[:, 0:256] if j < 2 else window[:, 128:384]


def head_masks(off):
    lane = lax.broadcasted_iota(jnp.int32, (128, 256), 1)
    masks = []
    for j in range(4):
        low = off + HEAD * j - (128 if j >= 2 else 0)
        masks.append(jnp.where((lane >= low) & (lane < low + HEAD), 1.0, 0.0).astype(BF16))
    return masks


def join(parts):
    left, right = parts[0] + parts[1], parts[2] + parts[3]
    return jnp.concatenate(
        [left[:, 0:128], left[:, 128:256] + right[:, 0:128], right[:, 128:256]], axis=1
    )


def forward4(q, k, v, masks, live):
    probs, outs = [], []
    for j in range(4):
        scores = dot_nt(half(q, j) * masks[j], half(k, j)) * SCALE
        if live is not None:
            scores = jnp.where(live, scores, -1e30)
        expo = jnp.exp(scores - jnp.max(scores, axis=-1, keepdims=True))
        prob = expo * (1.0 / jnp.sum(expo, axis=-1, keepdims=True))
        probs.append(prob)
        outs.append(dot(prob.astype(BF16), half(v, j) * masks[j]))
    return join(outs), probs


def backward4(g, q, k, v, probs, masks):
    dqs, dks, dvs = [], [], []
    for j in range(4):
        prob = probs[j]
        gh = half(g, j) * masks[j]
        dvs.append(dot_tn(prob.astype(BF16), gh))
        gp = dot_nt(gh, half(v, j))
        gs = prob * (gp - jnp.sum(gp * prob, axis=-1, keepdims=True))
        low = (gs * SCALE).astype(BF16)
        dqs.append(dot(low, half(k, j) * masks[j]))
        dks.append(dot_tn(low, half(q, j) * masks[j]))
    return join(dqs), join(dks), join(dvs)


def remote(src, dst, ssem, rsem, dp, s):
    return pltpu.make_async_remote_copy(
        src_ref=src, dst_ref=dst, send_sem=ssem, recv_sem=rsem,
        device_id=(dp, s), device_id_type=MESH,
    )


def m16(value):
    return pl.multiple_of(value, 16)


def kernel(
    len_ref, qkv, w, cot, bo, gqkv, gw,
    acc, prs, sob, wp, wr, wm, wf, so, cy, cz, c32, pj, to32, tob, ty, tf, gp32, gpb,
    gs, gr, gz, gf, pw, crv, kr, xr, zr, zb, fr, fs, fy, fd, gwf,
    wy_s, wy_r, wzr_s, wzr_r, wzl_s, wzl_r, wd_s, wd_r, cy_s, cy_r, cz_s, cz_r,
    sz_s, sz_r, sy_s, sy_r, ty_s, ty_r, tz_s, tz_r, gy_s, gy_r, gz_s, gz_r,
    pc_s, pc_r, px_s, px_r, pz_s, pz_r, py_s, py_r, pd_s, pd_r,
):
    dp, s = lax.axis_index("dp"), lax.axis_index("seq")
    y, z = lax.rem(s, NY), lax.div(s, NY)
    c, x = lax.rem(dp, NC), lax.div(dp, NC)
    sib = x * NC + (1 - c)
    sent = []

    def at_y(k):
        return lax.rem(y + k + NY, NY)

    def at_z(k):
        return lax.rem(z + k + NZ, NZ)

    def at_x(k):
        return lax.rem(x + k + NX, NX)

    def send(src, dst, ssem, rsem, dp_to, s_to):
        copy = remote(src, dst, ssem, rsem, dp_to, s_to)
        copy.start()
        sent.append(copy)

    def arrived(dst, ssem, rsem):
        remote(dst, dst, ssem, rsem, dp, s).wait_recv()

    barrier = pltpu.get_barrier_semaphore()
    for k in range(1, NY):
        pl.semaphore_signal(barrier, inc=1, device_id=(dp, z * NY + at_y(k)), device_id_type=MESH)
    for k in range(1, NZ):
        pl.semaphore_signal(barrier, inc=1, device_id=(dp, at_z(k) * NY + y), device_id_type=MESH)
    for k in range(1, NX * NC):
        pl.semaphore_signal(
            barrier, inc=1, device_id=(lax.rem(dp + k, NX * NC), s), device_id_type=MESH
        )

    wrow = w[...].astype(F32)
    for g in range(NY):
        piece = jnp.concatenate(
            [wrow[:, 288 * g + WIDTH * i: 288 * g + WIDTH * i + 288] for i in range(3)]
            + [jnp.zeros((36, 160), F32)], axis=1
        )
        piece = jnp.concatenate([piece, jnp.zeros((12, 1024), F32)], axis=0).astype(BF16)
        wp[g, 0] = piece[:, 0:512]
        wp[g, 1] = piece[:, 512:1024]
    cy[y] = cot[:, pl.ds(pl.multiple_of(256 * y, 128), 384)]
    wr[y] = wp[y, c]

    pl.semaphore_wait(barrier, NY + NZ + NX * NC - 3)
    for k in range(1, NY):
        to = at_y(k)
        send(wp.at[to, c], wr.at[y], wy_s.at[k - 1], wy_r.at[k - 1], dp, z * NY + to)
    for k in range(1, NY):
        to = at_y(k)
        send(
            cot.at[:, pl.ds(pl.multiple_of(256 * to, 128), 384)], cy.at[y],
            cy_s.at[k - 1], cy_r.at[k - 1], dp, z * NY + to,
        )

    acc[...] = jnp.zeros_like(acc)

    def spatial_forward(group):
        at = pl.multiple_of(256 * group, 128)
        q, k, v = (qkv[:, pl.ds(at + WIDTH * i, 384)] for i in range(3))
        out, probs = forward4(q, k, v, head_masks(32 * group), None)
        acc[:, pl.ds(at, 384)] += out
        for j in range(4):
            prs[4 * group + j] = probs[j]

    def block(k):
        return wf.at[c, pl.ds(m16(144 * at_z(k)), 144)]

    def to_sibling(k, order):
        send(block(k), block(k), wd_s.at[order], wd_r.at[order], sib, s)

    def ring(step):
        if step > 0:
            arrived(block(-step), wzr_s.at[step - 1], wzr_r.at[step - 1])
        if step < 4:
            send(block(-step), block(-step), wzr_s.at[step], wzr_r.at[step], dp, at_z(1) * NY + y)
        if 0 < step < 4:
            arrived(block(step), wzl_s.at[step - 1], wzl_r.at[step - 1])
        if step < 3:
            send(block(step), block(step), wzl_s.at[step], wzl_r.at[step], dp, at_z(-1) * NY + y)
        to_sibling(-step, step)
        if 0 < step < 4:
            to_sibling(step, 4 + step)

    spatial_forward(0)
    for k in range(1, NY):
        arrived(wr.at[at_y(-k)], wy_s.at[k - 1], wy_r.at[k - 1])
    for i in range(NY):
        wm[36 * i: 36 * i + 48, :] = wr[i].astype(F32)
    wf[c, pl.ds(m16(144 * z), 144)] = wm[0:144, :].astype(BF16)
    ring(0)
    spatial_forward(1)
    ring(1)
    spatial_forward(2)
    spatial_forward(3)
    ring(2)
    sob[...] = acc[:, 0:WIDTH].astype(BF16)
    for k in range(1, NZ):
        to = at_z(k)
        send(
            sob.at[pl.ds(m16(16 * to), 16)], so.at[z, y],
            sz_s.at[k - 1], sz_r.at[k - 1], dp, to * NY + y,
        )
    so[z, y] = sob[pl.ds(m16(16 * z), 16), :]
    for k in range(1, NY):
        arrived(cy.at[at_y(-k)], cy_s.at[k - 1], cy_r.at[k - 1])
    for k in range(1, NZ):
        to = at_z(k)
        send(
            cy.at[:, pl.ds(m16(16 * to), 16)], cz.at[z],
            cz_s.at[k - 1], cz_r.at[k - 1], dp, to * NY + y,
        )
    cz[z] = cy[:, pl.ds(m16(16 * z), 16), :]
    ring(3)
    for k in range(1, NZ):
        arrived(so.at[at_z(-k), y], sz_s.at[k - 1], sz_r.at[k - 1])
    for k in range(1, NY):
        to = at_y(k)
        send(so.at[:, y], so.at[:, y], sy_s.at[k - 1], sy_r.at[k - 1], dp, z * NY + to)
    ring(4)
    other = 1 - c
    for order, k in enumerate((0, -1, -2, -3, -4, 1, 2, 3)):
        arrived(
            wf.at[other, pl.ds(m16(144 * at_z(k)), 144)], wd_s.at[order], wd_r.at[order]
        )

    def project(at):
        rows = so[:, at].reshape(128, WIDTH)
        first = dot(rows, wf[0])
        second = dot(rows, wf[1, :, 0:384])
        for i in range(NZ):
            place = pl.ds(m16((NY * i + at) * 16), 16)
            for t in range(4):
                pj[t, place] = first[16 * i: 16 * i + 16, 128 * t: 128 * t + 128]
            for t in range(3):
                pj[4 + t, place] = second[16 * i: 16 * i + 16, 128 * t: 128 * t + 128]

    project(y)
    for k in range(1, NY):
        arrived(so.at[:, at_y(-k)], sy_s.at[k - 1], sy_r.at[k - 1])
        project(at_y(-k))

    for k in range(1, NZ):
        arrived(cz.at[at_z(-k)], cz_s.at[k - 1], cz_r.at[k - 1])
    g_in = cz[...].reshape(512, 384).astype(F32)
    turned = g_in
    for k in range(1, NY):
        turned = jnp.where(y == k, pltpu.roll(g_in, 384 - 32 * k, 1), turned)
    for t in range(3):
        c32[t] = turned[:, 128 * t: 128 * t + 128]

    length = len_ref[0]
    row = lax.broadcasted_iota(jnp.int32, (128, 128), 0)
    col = lax.broadcasted_iota(jnp.int32, (128, 128), 1)
    live = ((row >> 5) == (col >> 5)) & ((col & 31) < length)
    masks = head_masks(0)

    def temporal(b, carry):
        def rows_of(ref, first):
            return jnp.concatenate(
                [
                    jnp.concatenate(
                        [ref[t, pl.ds(4 * b + i, 32, stride=16), :] for i in range(4)], axis=0
                    )
                    for t in range(first, first + 3)
                ],
                axis=1,
            )

        q = rows_of(pj, 0).astype(BF16)
        k = pltpu.roll(rows_of(pj, 2), 384 - 32, 1).astype(BF16)
        v = pltpu.roll(rows_of(pj, 4), 384 - 64, 1).astype(BF16)
        g = rows_of(c32, 0).astype(BF16)
        out, probs = forward4(q, k, v, masks, live)
        dq, dk, dv = backward4(g, q, k, v, probs, masks)
        dk, dv = pltpu.roll(dk, 32, 1), pltpu.roll(dv, 64, 1)
        packed = jnp.concatenate(
            [dq[:, 0:256], dq[:, 256:384] + dk[:, 0:128], dk[:, 128:256],
             dk[:, 256:384] + dv[:, 0:128], dv[:, 128:384]], axis=1
        )
        for i in range(4):
            place = pl.ds(4 * b + i, 32, stride=16)
            for t in range(3):
                to32[t, place, :] = out[32 * i: 32 * i + 32, 128 * t: 128 * t + 128]
            for t in range(7):
                gp32[t, place, :] = packed[32 * i: 32 * i + 32, 128 * t: 128 * t + 128]
        return carry

    lax.fori_loop(0, 4, temporal, 0)

    for t in range(7):
        gpb[:, :, :, 128 * t: 128 * t + 128] = gp32[t].astype(BF16).reshape(NZ, NY, 16, 128)
    gpb[:, :, :, 896:1024] = jnp.zeros((NZ, NY, 16, 128), BF16)

    def back(to):
        rows = gpb[:, to].reshape(128, 1024)
        part = dot_nt(rows[:, 0:512], wf[0]) + dot_nt(rows[:, 512:896], wf[1, :, 0:384])
        gs[to] = part.astype(BF16).reshape(NZ, 16, WIDTH)

    for k in range(1, NY):
        to = at_y(k)
        back(to)
        send(gs.at[to], gr.at[k - 1], gy_s.at[k - 1], gy_r.at[k - 1], dp, z * NY + to)
    back(y)

    t_out = jnp.concatenate([to32[t] for t in range(3)], axis=1)
    turned = t_out
    for k in range(1, NY):
        turned = jnp.where(y == k, pltpu.roll(t_out, 32 * k, 1), turned)
    tob[...] = turned.astype(BF16).reshape(NZ, NY, 16, 384)
    for k in range(1, NY):
        to = at_y(k)
        send(tob.at[:, to], ty.at[y], ty_s.at[k - 1], ty_r.at[k - 1], dp, z * NY + to)
    ty[y] = tob[:, y]

    def weight_chunk(i, carry):
        at = pl.multiple_of(128 * i, 128)
        part = dot_tn(
            so[:, :, :, pl.ds(at, 128)].reshape(512, 128), gpb[...].reshape(512, 1024)
        ).astype(BF16)
        pw[0, pl.ds(at, 128)] = part[:, 0:512]
        pw[1, pl.ds(at, 128)] = part[:, 512:1024]
        return carry

    lax.fori_loop(0, 9, weight_chunk, 0)
    send(pw.at[1 - c], crv, pc_s, pc_r, sib, s)

    for k in range(1, NY):
        arrived(gr.at[k - 1], gy_s.at[k - 1], gy_r.at[k - 1])
    total = gs[y].astype(F32)
    for k in range(1, NY):
        total = total + gr[k - 1].astype(F32)
    gz[...] = total.astype(BF16)
    for k in range(1, NZ):
        to = at_z(k)
        send(gz.at[to], gf.at[z], gz_s.at[k - 1], gz_r.at[k - 1], dp, to * NY + y)
    gf[z] = gz[z]

    arrived(crv, pc_s, pc_r)
    kr[...] = (pw[c].astype(F32) + crv[...].astype(F32)).astype(BF16)
    for k in range(1, NX):
        to = at_x(k)
        send(
            kr.at[:, pl.ds(pl.multiple_of(128 * to, 128), 128)], xr.at[k - 1],
            px_s.at[k - 1], px_r.at[k - 1], to * NC + c, s,
        )

    for k in range(1, NY):
        arrived(ty.at[at_y(-k)], ty_s.at[k - 1], ty_r.at[k - 1])
    for k in range(1, NZ):
        to = at_z(k)
        send(ty.at[:, to], tf.at[z], tz_s.at[k - 1], tz_r.at[k - 1], dp, to * NY + y)
    tf[z] = ty[:, z]

    for k in range(1, NZ):
        arrived(gf.at[at_z(-k)], gz_s.at[k - 1], gz_r.at[k - 1])
    grad = (cot[...].astype(F32) + gf[...].reshape(128, WIDTH).astype(F32)).astype(BF16)
    sob2 = grad
    gf[...] = sob2.reshape(NZ, 16, WIDTH)
    acc[...] = jnp.zeros_like(acc)

    def spatial_backward(group, carry):
        at = pl.multiple_of(256 * group, 128)
        q, k, v = (qkv[:, pl.ds(at + WIDTH * i, 384)] for i in range(3))
        g = gf[:, :, pl.ds(at, 384)].reshape(128, 384)
        probs = [prs[4 * group + j] for j in range(4)]
        grads = backward4(g, q, k, v, probs, head_masks(32 * group))
        for i in range(3):
            acc[:, pl.ds(at + WIDTH * i, 384)] += grads[i]
        return carry

    lax.fori_loop(0, 2, spatial_backward, 0)

    for k in range(1, NX):
        arrived(xr.at[k - 1], px_s.at[k - 1], px_r.at[k - 1])
    total = kr[:, pl.ds(pl.multiple_of(128 * x, 128), 128)].astype(F32)
    for k in range(1, NX):
        total = total + xr[k - 1].astype(F32)
    zr[...] = total.astype(BF16).reshape(NZ, 144, 128)
    for k in range(1, NZ):
        to = at_z(k)
        send(zr.at[to], zb.at[z], pz_s.at[k - 1], pz_r.at[k - 1], dp, to * NY + y)
    zb[z] = zr[z]

    lax.fori_loop(2, 4, spatial_backward, 0)

    for k in range(1, NZ):
        arrived(zb.at[at_z(-k)], pz_s.at[k - 1], pz_r.at[k - 1])
    total = zb[0].astype(F32)
    for i in range(1, NZ):
        total = total + zb[i].astype(F32)
    fr[0:144, :] = total
    fr[144:160, :] = jnp.zeros((16, 128), F32)
    for i in range(NY):
        fs[i] = fr[36 * i: 36 * i + 48, :].astype(BF16)
    for k in range(1, NY):
        to = at_y(k)
        send(fs.at[to], fy.at[y], py_s.at[k - 1], py_r.at[k - 1], dp, z * NY + to)
    fy[y] = fs[y]

    gqkv[...] = acc[...].astype(BF16)
    for k in range(1, NZ):
        arrived(tf.at[at_z(-k)], tz_s.at[k - 1], tz_r.at[k - 1])
    acc[:, 0:WIDTH] = sob[...].astype(F32)
    for i in range(NY):
        acc[:, 256 * i: 256 * i + 384] += window_of(tf, i)
    bo[...] = acc[:, 0:WIDTH].astype(BF16)

    for k in range(1, NY):
        arrived(fy.at[at_y(-k)], py_s.at[k - 1], py_r.at[k - 1])
    n = NX * NC
    for k in range(1, n):
        to = lax.rem(dp + k, n)
        send(fy, fd.at[dp], pd_s.at[k - 1], pd_r.at[k - 1], to, s)
    fd[dp] = fy[...]
    for k in range(1, n):
        arrived(fd.at[lax.rem(dp + n - k, n)], pd_s.at[k - 1], pd_r.at[k - 1])
    gwf[...] = jnp.zeros_like(gwf)
    lane = lax.broadcasted_iota(jnp.int32, (48, 384), 1)
    for g in range(NY):
        for i in range(3):
            tiles = [2 * i + t for t in range(3)]
            window = jnp.concatenate(
                [fd[2 * (t % 4) + t // 4, g].astype(F32) for t in tiles], axis=1
            )
            if i > 0:
                window = pltpu.roll(window, 384 - 32 * i, 1)
            window = jnp.where(lane < 288, window, 0.0)
            if g > 0:
                window = pltpu.roll(window, 32 * g, 1)
            at = WIDTH * i + 256 * g
            gwf[:, at: at + 384] += window
    picked = jnp.zeros((48, 432), F32)
    for d in range(n):
        picked = jnp.where(dp == d, gwf[:, 432 * d: 432 * d + 432], picked)
    gw[...] = picked[0:36].astype(BF16)

    for copy in sent:
        copy.wait_send()


def window_of(ref, i):
    return ref[:, i].reshape(128, 384).astype(F32)


def local(spatial_qkv, lengths, w_qkv, cotangent):
    frames, patches = spatial_qkv.shape[1], spatial_qkv.shape[2]
    vmem = pl.BlockSpec(memory_space=pltpu.VMEM)
    dma = pltpu.SemaphoreType.DMA

    def bf(*shape):
        return pltpu.VMEM(shape, BF16)

    def fl(*shape):
        return pltpu.VMEM(shape, F32)

    out = pl.pallas_call(
        kernel,
        out_shape=(
            jax.ShapeDtypeStruct((patches, WIDTH), BF16),
            jax.ShapeDtypeStruct((patches, 3 * WIDTH), BF16),
            jax.ShapeDtypeStruct((36, 432), BF16),
        ),
        in_specs=[pl.BlockSpec(memory_space=pltpu.SMEM), vmem, vmem, vmem],
        out_specs=(vmem, vmem, vmem),
        scratch_shapes=[
            fl(128, 3 * WIDTH),
            fl(16, 128, 128),
            bf(128, WIDTH),
            bf(4, 2, 48, 512),
            bf(4, 48, 512),
            fl(160, 512),
            bf(2, WIDTH, 512),
            bf(8, 4, 16, WIDTH),
            bf(4, 128, 384),
            bf(8, 4, 16, 384),
            fl(3, 512, 128),
            fl(7, 512, 128),
            fl(3, 512, 128),
            bf(8, 4, 16, 384),
            bf(4, 8, 16, 384),
            bf(8, 4, 16, 384),
            fl(7, 512, 128),
            bf(8, 4, 16, 1024),
            bf(4, 8, 16, WIDTH),
            bf(3, 8, 16, WIDTH),
            bf(8, 16, WIDTH),
            bf(8, 16, WIDTH),
            bf(2, WIDTH, 512),
            bf(WIDTH, 512),
            bf(WIDTH, 512),
            bf(3, WIDTH, 128),
            bf(8, 144, 128),
            bf(8, 144, 128),
            fl(160, 128),
            bf(4, 48, 128),
            bf(4, 48, 128),
            bf(8, 4, 48, 128),
            fl(48, 3 * WIDTH),
            dma((3,)), dma((3,)), dma((4,)), dma((4,)), dma((3,)), dma((3,)), dma((8,)), dma((8,)),
            dma((3,)), dma((3,)), dma((7,)), dma((7,)),
            dma((7,)), dma((7,)), dma((3,)), dma((3,)),
            dma((3,)), dma((3,)), dma((7,)), dma((7,)),
            dma((3,)), dma((3,)), dma((7,)), dma((7,)),
            dma, dma, dma((3,)), dma((3,)), dma((7,)), dma((7,)),
            dma((3,)), dma((3,)), dma((7,)), dma((7,)),
        ],
        compiler_params=pltpu.CompilerParams(
            collective_id=0, has_side_effects=True, vmem_limit_bytes=50 * 1024 * 1024
        ),
    )(
        lengths, spatial_qkv.reshape(patches, 3 * WIDTH), w_qkv,
        cotangent.reshape(patches, WIDTH),
    )
    return (
        out[0].reshape(1, frames, patches, WIDTH),
        out[1].reshape(1, frames, patches, 3 * WIDTH),
        out[2],
    )


def solution(mesh):
    in_specs = (P("dp", "seq", None, None), P("dp"), P("seq", None), P("dp", "seq", None, None))
    out_specs = (P("dp", "seq", None, None), P("dp", "seq", None, None), P("seq", "dp"))
    return jax.shard_map(local, mesh=mesh, in_specs=in_specs, out_specs=out_specs, check_vma=False)
```

time: 547 us -> 118 us (0.22); the launches traced: 536 us -> 118 us
  waiting for transfers between devices: 158 us -> 0 us
  blocking collectives: 137 us -> 0 us
  Pallas kernels: 0 us -> 111 us
  starting transfers between devices: 85.9 us -> 0 us
  local copies, waits for them, and re-layouts: 89 us -> 5.32 us
  matrix products: 35.5 us -> 0 us
  between operations: 16.1 us -> 1.3 us
  other arithmetic: 13.6 us -> 0 us
    unnamed x1 -> x0, blocking collectives: 137 us -> none
    pallas_call x0 -> x1, Pallas kernels: none -> 111 us  [local(): pl.pallas_call(kernel, out_shape=(jax.ShapeDtypeStruct((patches, WIDTH),...]
    all_gather x1 -> x0, waiting for transfers between devices: 74.6 us -> none  [local(): w_full = lax.all_gather(w_qkv, 'seq', axis=0, tiled=True)]
    unnamed x11 -> x0, waiting for transfers between devices: 62.7 us -> none
    unnamed x60 -> x9, local copies, waits for them, and re-layouts: 60.8 us -> 5.32 us
    unnamed x9 -> x0, starting transfers between devices: 46.5 us -> none
    all_to_all x5 -> x0, starting transfers between devices: 39.3 us -> none  [the longest x1 12 us: local(): lax.all_to_all(cotangent, 'seq', split_axis=2, concat_axis=1, tiled=True)]
    dot_general x13 -> x0, matrix products: 32 us -> none  [the longest x1 5.81 us: project_back(): lax.dot_general(rows, weight, (((1,), (1,)), ((), ())), preferred_element...]
  transfers between devices with their start and end apart: 15 -> 0, of which waited for: 6 -> 0; matrix products, arithmetic and copies ran while one was open for 44% -> 0% of each run, Pallas kernels for 0% -> 0%
where the time goes in v1:
time: 118 us
  Pallas kernels  111 us (94%)
  local copies, waits for them, and re-layouts  5.32 us (5%)
  between operations  1.3 us (1%)
    pallas_call x1, Pallas kernels, local(): pl.pallas_call(kernel, out_shape=(jax.ShapeDtypeStruct((patches, WIDTH),...  111 us
    unnamed x9, local copies, waits for them, and re-layouts  5.32 us

profile of v1, /device:TPU:1, one launch (start us, length us, event | category | flops | bytes accessed | tf_op | source)
XLA Modules:
  0.0 117.9 jit_solution(14131733592797604476)
XLA Ops:
  1.3 0.0 copy-start
  1.3 1.2 copy-done
  2.4 0.0 copy-start.1
  2.4 1.0 copy-done.1
  3.4 0.0 copy-start.2
  3.4 1.0 copy-done.2
  4.4 111.3 %shard_map.67 = (bf16[128,1152]{1,0:T(8,128)(2,1)S(1)}, bf16[128,3456]{1,0:T(8,128)(2,1)S(1)}, bf16[36,432]{1,0:T(8,128)(2,1)S(1)}) custom-call(s32[1]{0:T(128)S(6)} %copy.10.len_ref, bf16[128,3456]{1,0:T(8,128)(2,1)S(1)} %bitcast.5, bf16[36,3456]{1,0:T(8,128)(2,1)S(1)} %copy-done.2, bf16[128,1152]{1,0:T(8,128)(2,1)S(1)} %bitcast.7), custom_call_target="tpu_custom_call" | custom-call | tf_op jit(solution)/shard_map/pallas_call | solution.py:452
  115.7 0.7 copy.11
  116.4 0.9 copy.12
  117.3 0.6 copy.13
Async XLA Ops:
  1.3 1.2 copy-start
  2.4 1.0 copy-start.1
  3.4 1.0 copy-start.2

commit v2 on v1

v2 whole, which is shorter than its diff:
```python
import jax
import jax.numpy as jnp
from jax import lax
from jax.experimental import pallas as pl
from jax.experimental.pallas import tpu as pltpu
from jax.sharding import PartitionSpec as P

HEADS = 16
WIDTH = 1152
HEAD = 72
NY, NZ, NX, NC = 4, 8, 4, 2
MESH = pl.DeviceIdType.MESH
F32, BF16 = jnp.float32, jnp.bfloat16
SCALE = HEAD ** (-0.5)


def dot(a, b):
    return lax.dot_general(a, b, (((1,), (0,)), ((), ())), preferred_element_type=F32)


def dot_nt(a, b):
    return lax.dot_general(a, b, (((1,), (1,)), ((), ())), preferred_element_type=F32)


def dot_tn(a, b):
    return lax.dot_general(a, b, (((0,), (0,)), ((), ())), preferred_element_type=F32)


def half(window, j):
    return window[:, 0:256] if j < 2 else window[:, 128:384]


def head_masks(off):
    lane = lax.broadcasted_iota(jnp.int32, (128, 256), 1)
    masks = []
    for j in range(4):
        low = off + HEAD * j - (128 if j >= 2 else 0)
        masks.append(jnp.where((lane >= low) & (lane < low + HEAD), 1.0, 0.0).astype(BF16))
    return masks


def join(parts):
    left, right = parts[0] + parts[1], parts[2] + parts[3]
    return jnp.concatenate(
        [left[:, 0:128], left[:, 128:256] + right[:, 0:128], right[:, 128:256]], axis=1
    )


def forward4(q, k, v, masks, live):
    probs, outs = [], []
    for j in range(4):
        scores = dot_nt(half(q, j) * masks[j], half(k, j)) * SCALE
        if live is not None:
            scores = jnp.where(live, scores, -1e30)
        expo = jnp.exp(scores - jnp.max(scores, axis=-1, keepdims=True))
        prob = expo * (1.0 / jnp.sum(expo, axis=-1, keepdims=True))
        probs.append(prob)
        outs.append(dot(prob.astype(BF16), half(v, j) * masks[j]))
    return join(outs), probs


def backward4(g, q, k, v, probs, masks):
    dqs, dks, dvs = [], [], []
    for j in range(4):
        prob = probs[j]
        gh = half(g, j) * masks[j]
        dvs.append(dot_tn(prob.astype(BF16), gh))
        gp = dot_nt(gh, half(v, j))
        gs = prob * (gp - jnp.sum(gp * prob, axis=-1, keepdims=True))
        low = (gs * SCALE).astype(BF16)
        dqs.append(dot(low, half(k, j) * masks[j]))
        dks.append(dot_tn(low, half(q, j) * masks[j]))
    return join(dqs), join(dks), join(dvs)


def remote(src, dst, ssem, rsem, dp, s):
    return pltpu.make_async_remote_copy(
        src_ref=src, dst_ref=dst, send_sem=ssem, recv_sem=rsem,
        device_id=(dp, s), device_id_type=MESH,
    )


def m16(value):
    return pl.multiple_of(value, 16)


Z_ORDER = (1, 7, 2, 6, 3, 5, 4)
BLOCK = 144
CHUNK = 384


def placed(group, tile):
    found = set()
    for part in range(3):
        low = max(128 * tile, 288 * part)
        high = min(128 * tile + 128, 288 * part + 288)
        if low < high:
            shift = WIDTH * part + 288 * group - 288 * part
            found |= set(range((low + shift) // 432, (high - 1 + shift) // 432 + 1))
    return sorted(found)


def tile_owner(tile):
    return 2 * (tile % 4) + tile // 4


def kernel(
    len_ref, qkv_h, w, cot_h, bo, gqkv, gw,
    qkv, cot, acc, prs, prt, blk, sob, wp, wr, wm, wf, so, cy, cz, c32, pj, to32, tob, ty, tf,
    gp32, gpb, gs, gr, gz, gf, grad, pw, crv, kr, xr, zr, zb, fr, fs, fy, fd, gwf,
    in_s, wy_s, wy_r, wz_s, wz_r, wx_s, wx_r, wd_s, wd_r, cy_s, cy_r, cz_s, cz_r,
    sz_s, sz_r, sy_s, sy_r, ty_s, ty_r, tz_s, tz_r, gy_s, gy_r, gz_s, gz_r,
    pc_s, pc_r, px_s, px_r, pz_s, pz_r, py_s, py_r, pd_s, pd_r,
):
    dp, s = lax.axis_index("dp"), lax.axis_index("seq")
    y, z = lax.rem(s, NY), lax.div(s, NY)
    c, x = lax.rem(dp, NC), lax.div(dp, NC)
    sib = x * NC + (1 - c)
    mine = 4 * c + x
    sent = []

    def at_y(k):
        return lax.rem(y + k + NY, NY)

    def at_z(k):
        return lax.rem(z + k + NZ, NZ)

    def at_x(k):
        return lax.rem(x + k + NX, NX)

    def send(src, dst, ssem, rsem, dp_to, s_to):
        copy = remote(src, dst, ssem, rsem, dp_to, s_to)
        copy.start()
        sent.append(copy)

    def arrived(dst, ssem, rsem):
        remote(dst, dst, ssem, rsem, dp, s).wait_recv()

    barrier = pltpu.get_barrier_semaphore()
    for k in range(1, NY):
        pl.semaphore_signal(barrier, inc=1, device_id=(dp, z * NY + at_y(k)), device_id_type=MESH)
    for k in range(1, NZ):
        pl.semaphore_signal(barrier, inc=1, device_id=(dp, at_z(k) * NY + y), device_id_type=MESH)
    for k in range(1, NX * NC):
        pl.semaphore_signal(
            barrier, inc=1, device_id=(lax.rem(dp + k, NX * NC), s), device_id_type=MESH
        )
    qkv_in = pltpu.make_async_copy(qkv_h, qkv, in_s.at[0])
    cot_in = pltpu.make_async_copy(cot_h, cot, in_s.at[1])
    qkv_in.start()
    cot_in.start()

    wrow = w[...].astype(F32)
    for g in range(NY):
        piece = jnp.concatenate(
            [wrow[:, 288 * g + WIDTH * i: 288 * g + WIDTH * i + 288] for i in range(3)]
            + [jnp.zeros((36, 160), F32)], axis=1
        )
        piece = jnp.concatenate([piece, jnp.zeros((12, 1024), F32)], axis=0).astype(BF16)
        for t in range(8):
            wp[g, t] = piece[:, 128 * t: 128 * t + 128]
    wr[y] = wp[y, mine]
    acc[...] = jnp.zeros_like(acc)
    fd[...] = jnp.zeros_like(fd)

    def spatial_forward(group):
        at = pl.multiple_of(256 * group, 128)
        q, k, v = (qkv[:, pl.ds(at + WIDTH * i, 384)] for i in range(3))
        out, probs = forward4(q, k, v, head_masks(32 * group), None)
        acc[:, pl.ds(at, 384)] += out
        for j in range(4):
            prs[4 * group + j] = probs[j]

    qkv_in.wait()
    cot_in.wait()
    spatial_forward(0)
    cy[y] = cot[:, pl.ds(pl.multiple_of(256 * y, 128), 384)]

    pl.semaphore_wait(barrier, NY + NZ + NX * NC - 3)
    for k in range(1, NY):
        to = at_y(k)
        send(wp.at[to, mine], wr.at[y], wy_s.at[k - 1], wy_r.at[k - 1], dp, z * NY + to)
    for k in range(1, NY):
        to = at_y(k)
        send(
            cot.at[:, pl.ds(pl.multiple_of(256 * to, 128), 384)], cy.at[y],
            cy_s.at[k - 1], cy_r.at[k - 1], dp, z * NY + to,
        )
    spatial_forward(1)
    spatial_forward(2)
    spatial_forward(3)
    sob[...] = acc[:, 0:WIDTH].astype(BF16)

    for k in range(1, NY):
        arrived(wr.at[at_y(-k)], wy_s.at[k - 1], wy_r.at[k - 1])
    for i in range(NY):
        wm[36 * i: 36 * i + 48, :] = wr[i].astype(F32)
    wf[mine, pl.ds(m16(BLOCK * z), BLOCK)] = wm[0:BLOCK, :].astype(BF16)

    def rows(k):
        return pl.ds(m16(BLOCK * at_z(k)), BLOCK)

    def weight_x(order, k):
        for i in range(1, NX):
            block = wf.at[mine, rows(k)]
            send(block, block, wx_s.at[order, i - 1], wx_r.at[order, i - 1], at_x(i) * NC + c, s)

    def spread_y(order, k):
        for i in range(1, NY):
            block = so.at[at_z(k), y]
            send(block, block, sy_s.at[order, i - 1], sy_r.at[order, i - 1], dp, z * NY + at_y(i))

    for k in Z_ORDER:
        block = wf.at[mine, rows(0)]
        send(block, block, wz_s.at[k - 1], wz_r.at[k - 1], dp, at_z(k) * NY + y)
    weight_x(0, 0)
    for k in Z_ORDER:
        to = at_z(k)
        send(
            sob.at[pl.ds(m16(16 * to), 16)], so.at[z, y],
            sz_s.at[k - 1], sz_r.at[k - 1], dp, to * NY + y,
        )
    so[z, y] = sob[pl.ds(m16(16 * z), 16), :]
    spread_y(0, 0)
    for order, k in enumerate(Z_ORDER):
        arrived(wf.at[mine, rows(-k)], wz_s.at[k - 1], wz_r.at[k - 1])
        weight_x(order + 1, -k)
        arrived(so.at[at_z(-k), y], sz_s.at[k - 1], sz_r.at[k - 1])
        spread_y(order + 1, -k)

    for k in range(1, NY):
        arrived(cy.at[at_y(-k)], cy_s.at[k - 1], cy_r.at[k - 1])
    for k in Z_ORDER:
        to = at_z(k)
        send(
            cy.at[:, pl.ds(m16(16 * to), 16)], cz.at[z],
            cz_s.at[k - 1], cz_r.at[k - 1], dp, to * NY + y,
        )
    cz[z] = cy[:, pl.ds(m16(16 * z), 16), :]

    for order, k in enumerate((0,) + Z_ORDER):
        for i in range(1, NX):
            arrived(
                wf.at[4 * c + at_x(-i), rows(-k)], wx_s.at[order, i - 1], wx_r.at[order, i - 1]
            )
        block = wf.at[pl.ds(4 * c, 4), rows(-k)]
        send(block, block, wd_s.at[order], wd_r.at[order], sib, s)
    for order, k in enumerate((0,) + Z_ORDER):
        for i in range(1, NY):
            arrived(so.at[at_z(-k), at_y(-i)], sy_s.at[order, i - 1], sy_r.at[order, i - 1])
    for order, k in enumerate((0,) + Z_ORDER):
        arrived(wf.at[pl.ds(4 - 4 * c, 4), rows(-k)], wd_s.at[order], wd_r.at[order])

    every = so[...].reshape(512, WIDTH)
    for t in range(4):
        if t < 3:
            pair = dot(every, jnp.concatenate([wf[2 * t], wf[2 * t + 1]], axis=1))
            pj[2 * t], pj[2 * t + 1] = pair[:, 0:128], pair[:, 128:256]
        else:
            pj[6] = dot(every, wf[6])

    length = len_ref[0]
    row = lax.broadcasted_iota(jnp.int32, (128, 128), 0)
    col = lax.broadcasted_iota(jnp.int32, (128, 128), 1)
    live = ((row >> 5) == (col >> 5)) & ((col & 31) < length)
    masks = head_masks(0)

    def rows_of(ref, first, b):
        return jnp.concatenate(
            [
                jnp.concatenate(
                    [ref[t, pl.ds(4 * b + i, 32, stride=16), :] for i in range(4)], axis=0
                )
                for t in range(first, first + 3)
            ],
            axis=1,
        )

    def temporal_forward(b, carry):
        q = rows_of(pj, 0, b).astype(BF16)
        k = pltpu.roll(rows_of(pj, 2, b), 384 - 32, 1).astype(BF16)
        v = pltpu.roll(rows_of(pj, 4, b), 384 - 64, 1).astype(BF16)
        blk[b, 0], blk[b, 1], blk[b, 2] = q, k, v
        out, probs = forward4(q, k, v, masks, live)
        for j in range(4):
            prt[b, j] = probs[j]
        for i in range(4):
            for t in range(3):
                to32[t, pl.ds(4 * b + i, 32, stride=16), :] = out[
                    32 * i: 32 * i + 32, 128 * t: 128 * t + 128
                ]
        return carry

    lax.fori_loop(0, 4, temporal_forward, 0)

    t_out = jnp.concatenate([to32[t] for t in range(3)], axis=1)
    turned = t_out
    for k in range(1, NY):
        turned = jnp.where(y == k, pltpu.roll(t_out, 32 * k, 1), turned)
    tob[...] = turned.astype(BF16).reshape(NZ, NY, 16, 384)
    for k in range(1, NY):
        to = at_y(k)
        send(tob.at[:, to], ty.at[y], ty_s.at[k - 1], ty_r.at[k - 1], dp, z * NY + to)
    ty[y] = tob[:, y]

    for k in Z_ORDER:
        arrived(cz.at[at_z(-k)], cz_s.at[k - 1], cz_r.at[k - 1])
    g_in = cz[...].reshape(512, 384).astype(F32)
    turned = g_in
    for k in range(1, NY):
        turned = jnp.where(y == k, pltpu.roll(g_in, 384 - 32 * k, 1), turned)
    for t in range(3):
        c32[t] = turned[:, 128 * t: 128 * t + 128]

    def temporal_backward(b, carry):
        q, k, v = blk[b, 0], blk[b, 1], blk[b, 2]
        g = rows_of(c32, 0, b).astype(BF16)
        dq, dk, dv = backward4(g, q, k, v, [prt[b, j] for j in range(4)], masks)
        dk, dv = pltpu.roll(dk, 32, 1), pltpu.roll(dv, 64, 1)
        packed = jnp.concatenate(
            [dq[:, 0:256], dq[:, 256:384] + dk[:, 0:128], dk[:, 128:256],
             dk[:, 256:384] + dv[:, 0:128], dv[:, 128:384]], axis=1
        )
        for i in range(4):
            for t in range(7):
                gp32[t, pl.ds(4 * b + i, 32, stride=16), :] = packed[
                    32 * i: 32 * i + 32, 128 * t: 128 * t + 128
                ]
        return carry

    lax.fori_loop(0, 4, temporal_backward, 0)

    for t in range(7):
        gpb[:, 128 * t: 128 * t + 128] = gp32[t].astype(BF16)
    gpb[:, 896:1024] = jnp.zeros((512, 128), BF16)

    def weight_chunk(i):
        at = CHUNK * i
        part = dot_tn(so[:, :, :, at: at + CHUNK].reshape(512, CHUNK), gpb[...]).astype(BF16)
        for t in range(8):
            pw[t, at: at + CHUNK] = part[:, 128 * t: 128 * t + 128]
        send(
            pw.at[pl.ds(4 - 4 * c, 4), at: at + CHUNK], crv.at[:, at: at + CHUNK],
            pc_s.at[i], pc_r.at[i], sib, s,
        )

    def back_chunk(i):
        at = CHUNK * i
        part = jnp.zeros((512, CHUNK), F32)
        for t in range(4):
            if t < 3:
                weight = jnp.concatenate(
                    [wf[2 * t, at: at + CHUNK], wf[2 * t + 1, at: at + CHUNK]], axis=1
                )
                part = part + dot_nt(gpb[:, 256 * t: 256 * t + 256], weight)
            else:
                part = part + dot_nt(gpb[:, 768:896], wf[6, at: at + CHUNK])
        gs[i] = part.astype(BF16).reshape(NZ, NY, 16, CHUNK)
        for k in range(1, NY):
            to = at_y(k)
            send(
                gs.at[i, :, to], gr.at[i, k - 1],
                gy_s.at[i, k - 1], gy_r.at[i, k - 1], dp, z * NY + to,
            )

    def weight_sum(i):
        at = CHUNK * i
        arrived(crv.at[:, at: at + CHUNK], pc_s.at[i], pc_r.at[i])
        kr[:, at: at + CHUNK] = (
            pw[pl.ds(4 * c, 4), at: at + CHUNK].astype(F32) + crv[:, at: at + CHUNK].astype(F32)
        ).astype(BF16)
        for k in range(1, NX):
            to = at_x(k)
            send(
                kr.at[to, at: at + CHUNK], xr.at[k - 1, at: at + CHUNK],
                px_s.at[i, k - 1], px_r.at[i, k - 1], to * NC + c, s,
            )

    def weight_z(i, blocks):
        at = CHUNK * i
        for k in range(1, NX):
            arrived(xr.at[k - 1, at: at + CHUNK], px_s.at[i, k - 1], px_r.at[i, k - 1])
        total = kr[x, at: at + CHUNK].astype(F32)
        for k in range(1, NX):
            total = total + xr[k - 1, at: at + CHUNK].astype(F32)
        zr[at: at + CHUNK] = total.astype(BF16)
        for b in blocks:
            @pl.when(z != b)
            def _():
                remote(
                    zr.at[BLOCK * b: BLOCK * b + BLOCK], zb.at[z],
                    pz_s.at[b], pz_r.at[z], dp, b * NY + y,
                ).start()

    def back_sum(i):
        for k in range(1, NY):
            arrived(gr.at[i, k - 1], gy_s.at[i, k - 1], gy_r.at[i, k - 1])
        total = gs[i, :, y].astype(F32)
        for k in range(1, NY):
            total = total + gr[i, k - 1].astype(F32)
        gz[i] = total.astype(BF16)
        for k in Z_ORDER:
            to = at_z(k)
            send(
                gz.at[i, to], gf.at[i, z], gz_s.at[i, k - 1], gz_r.at[i, k - 1], dp, to * NY + y
            )
        gf[i, z] = gz[i, z]

    def back_done(i):
        at = CHUNK * i
        for k in Z_ORDER:
            arrived(gf.at[i, at_z(-k)], gz_s.at[i, k - 1], gz_r.at[i, k - 1])
        grad[:, at: at + CHUNK] = (
            cot[:, at: at + CHUNK].astype(F32) + gf[i].reshape(128, CHUNK).astype(F32)
        ).astype(BF16)

    def spatial_backward(group):
        at = 256 * group
        q, k, v = (qkv[:, at + WIDTH * i: at + WIDTH * i + 384] for i in range(3))
        probs = [prs[4 * group + j] for j in range(4)]
        grads = backward4(grad[:, at: at + 384], q, k, v, probs, head_masks(32 * group))
        for i in range(3):
            acc[:, at + WIDTH * i: at + WIDTH * i + 384] += grads[i]

    weight_chunk(0)
    back_chunk(0)
    weight_chunk(1)
    weight_sum(0)
    weight_chunk(2)
    weight_sum(1)
    back_chunk(1)
    back_chunk(2)
    weight_sum(2)

    for k in range(1, NY):
        arrived(ty.at[at_y(-k)], ty_s.at[k - 1], ty_r.at[k - 1])
    for k in Z_ORDER:
        to = at_z(k)
        send(ty.at[:, to], tf.at[z], tz_s.at[k - 1], tz_r.at[k - 1], dp, to * NY + y)
    tf[z] = ty[:, z]
    acc[...] = jnp.zeros_like(acc)

    back_sum(0)
    weight_z(0, (0, 1))
    back_sum(1)
    weight_z(1, (2, 3, 4))
    back_sum(2)
    back_done(0)
    spatial_backward(0)
    weight_z(2, (5, 6, 7))
    back_done(1)
    spatial_backward(1)
    back_done(2)
    spatial_backward(2)
    spatial_backward(3)

    zb[z] = zr[pl.ds(m16(BLOCK * z), BLOCK)]
    for b in range(NZ):
        @pl.when(z != b)
        def _():
            arrived(zb.at[b], pz_s.at[b], pz_r.at[b])
    total = zb[0].astype(F32)
    for i in range(1, NZ):
        total = total + zb[i].astype(F32)
    fr[0:BLOCK, :] = total
    fr[BLOCK:160, :] = jnp.zeros((16, 128), F32)
    for i in range(NY):
        fs[i] = fr[36 * i: 36 * i + 48, :].astype(BF16)
    for k in range(1, NY):
        to = at_y(k)
        send(fs.at[to], fy.at[y], py_s.at[k - 1], py_r.at[k - 1], dp, z * NY + to)
    fy[y] = fs[y]

    gqkv[...] = acc[...].astype(BF16)
    for k in Z_ORDER:
        arrived(tf.at[at_z(-k)], tz_s.at[k - 1], tz_r.at[k - 1])
    acc[:, 0:WIDTH] = sob[...].astype(F32)
    for i in range(NY):
        acc[:, 256 * i: 256 * i + 384] += tf[:, i].reshape(128, 384).astype(F32)
    bo[...] = acc[:, 0:WIDTH].astype(BF16)

    for k in range(1, NY):
        arrived(fy.at[at_y(-k)], py_s.at[k - 1], py_r.at[k - 1])

    def moves(tile):
        return [
            (g, d) for g in range(NY) for d in placed(g, tile) if d != tile_owner(tile)
        ]

    def move(tile, g, d):
        return remote(fy.at[g], fd.at[tile, g], pd_s.at[g, d], pd_r.at[tile, g], d, s)

    for tile in range(7):
        @pl.when(dp == tile_owner(tile))
        def _():
            for g, d in moves(tile):
                move(tile, g, d).start()
    fd[mine] = fy[...]
    for d in range(NX * NC):
        @pl.when(dp == d)
        def _():
            for tile in range(7):
                for g, to in moves(tile):
                    if to == d:
                        arrived(fd.at[tile, g], pd_s.at[g, d], pd_r.at[tile, g])
    gwf[...] = jnp.zeros_like(gwf)
    lane = lax.broadcasted_iota(jnp.int32, (48, 384), 1)
    for g in range(NY):
        for i in range(3):
            window = jnp.concatenate(
                [fd[2 * i + t, g].astype(F32) for t in range(3)], axis=1
            )
            if i > 0:
                window = pltpu.roll(window, 384 - 32 * i, 1)
            window = jnp.where(lane < 288, window, 0.0)
            if g > 0:
                window = pltpu.roll(window, 32 * g, 1)
            at = WIDTH * i + 256 * g
            gwf[:, at: at + 384] += window
    picked = jnp.zeros((48, 432), F32)
    for d in range(NX * NC):
        picked = jnp.where(dp == d, gwf[:, 432 * d: 432 * d + 432], picked)
    gw[...] = picked[0:36].astype(BF16)

    for copy in sent:
        copy.wait_send()
    for b in range(NZ):
        @pl.when(z != b)
        def _():
            remote(
                zr.at[BLOCK * b: BLOCK * b + BLOCK], zb.at[z], pz_s.at[b], pz_r.at[z], dp, s
            ).wait_send()
    for tile in range(7):
        @pl.when(dp == tile_owner(tile))
        def _():
            for g, d in moves(tile):
                move(tile, g, d).wait_send()


def local(spatial_qkv, lengths, w_qkv, cotangent):
    frames, patches = spatial_qkv.shape[1], spatial_qkv.shape[2]
    vmem = pl.BlockSpec(memory_space=pltpu.VMEM)
    anywhere = pl.BlockSpec(memory_space=pltpu.HBM)
    dma = pltpu.SemaphoreType.DMA

    def bf(*shape):
        return pltpu.VMEM(shape, BF16)

    def fl(*shape):
        return pltpu.VMEM(shape, F32)

    out = pl.pallas_call(
        kernel,
        out_shape=(
            jax.ShapeDtypeStruct((patches, WIDTH), BF16),
            jax.ShapeDtypeStruct((patches, 3 * WIDTH), BF16),
            jax.ShapeDtypeStruct((36, 432), BF16),
        ),
        in_specs=[pl.BlockSpec(memory_space=pltpu.SMEM), anywhere, vmem, anywhere],
        out_specs=(vmem, vmem, vmem),
        scratch_shapes=[
            bf(128, 3 * WIDTH),
            bf(128, WIDTH),
            fl(128, 3 * WIDTH),
            fl(16, 128, 128),
            fl(4, 4, 128, 128),
            bf(4, 3, 128, 384),
            bf(128, WIDTH),
            bf(4, 8, 48, 128),
            bf(4, 48, 128),
            fl(160, 128),
            bf(8, WIDTH, 128),
            bf(8, 4, 16, WIDTH),
            bf(4, 128, 384),
            bf(8, 4, 16, 384),
            fl(3, 512, 128),
            fl(7, 512, 128),
            fl(3, 512, 128),
            bf(8, 4, 16, 384),
            bf(4, 8, 16, 384),
            bf(8, 4, 16, 384),
            fl(7, 512, 128),
            bf(512, 1024),
            bf(3, 8, 4, 16, CHUNK),
            bf(3, 3, 8, 16, CHUNK),
            bf(3, 8, 16, CHUNK),
            bf(3, 8, 16, CHUNK),
            bf(128, WIDTH),
            bf(8, WIDTH, 128),
            bf(4, WIDTH, 128),
            bf(4, WIDTH, 128),
            bf(3, WIDTH, 128),
            bf(WIDTH, 128),
            bf(8, BLOCK, 128),
            fl(160, 128),
            bf(4, 48, 128),
            bf(4, 48, 128),
            bf(8, 4, 48, 128),
            fl(48, 3 * WIDTH),
            dma((2,)), dma((3,)), dma((3,)), dma((7,)), dma((7,)),
            dma((8, 3)), dma((8, 3)), dma((8,)), dma((8,)),
            dma((3,)), dma((3,)), dma((7,)), dma((7,)),
            dma((7,)), dma((7,)), dma((8, 3)), dma((8, 3)),
            dma((3,)), dma((3,)), dma((7,)), dma((7,)),
            dma((3, 3)), dma((3, 3)), dma((3, 7)), dma((3, 7)),
            dma((3,)), dma((3,)), dma((3, 3)), dma((3, 3)), dma((8,)), dma((8,)),
            dma((3,)), dma((3,)), dma((4, 8)), dma((8, 4)),
        ],
        compiler_params=pltpu.CompilerParams(
            collective_id=0, has_side_effects=True, vmem_limit_bytes=50 * 1024 * 1024
        ),
    )(
        lengths, spatial_qkv.reshape(patches, 3 * WIDTH), w_qkv,
        cotangent.reshape(patches, WIDTH),
    )
    return (
        out[0].reshape(1, frames, patches, WIDTH),
        out[1].reshape(1, frames, patches, 3 * WIDTH),
        out[2],
    )


def solution(mesh):
    in_specs = (P("dp", "seq", None, None), P("dp"), P("seq", None), P("dp", "seq", None, None))
    out_specs = (P("dp", "seq", None, None), P("dp", "seq", None, None), P("seq", "dp"))
    return jax.shard_map(local, mesh=mesh, in_specs=in_specs, out_specs=out_specs, check_vma=False)
```

time: 118 us -> 94.6 us (0.80)
  Pallas kernels: 111 us -> 87.8 us
    pallas_call x1, Pallas kernels: 111 us -> 87.8 us  [local(): pl.pallas_call(kernel, out_shape=(jax.ShapeDtypeStruct((patches, WIDTH),...]
where the time goes in v2:
time: 94.6 us; the launch traced here: 94.5 us
  Pallas kernels  87.8 us (93%)
  local copies, waits for them, and re-layouts  5.32 us (6%)
  between operations  1.3 us (1%)
    pallas_call x1, Pallas kernels, local(): pl.pallas_call(kernel, out_shape=(jax.ShapeDtypeStruct((patches, WIDTH),...  87.8 us
    unnamed x9, local copies, waits for them, and re-layouts  5.32 us

profile of v2, /device:TPU:1, one launch (start us, length us, event | category | flops | bytes accessed | tf_op | source)
XLA Modules:
  0.0 94.5 jit_solution(7376963437992616295)
XLA Ops:
  1.3 0.0 copy-start
  1.3 1.2 %copy-done = bf16[1,1,128,3456]{3,2,1,0:T(8,128)(2,1)S(1)} copy-done((bf16[1,1,128,3456]{3,2,1,0:T(8,128)(2,1)S(1)}, bf16[1,1,128,3456]{3,2,1,0:T(8,128)(2,1)}, u32[]{:S(2)}) %copy-start) | copy-done | bytes 884760
  2.4 0.0 copy-start.1
  2.4 1.0 %copy-done.1 = bf16[1,1,128,1152]{3,2,1,0:T(8,128)(2,1)S(1)} copy-done((bf16[1,1,128,1152]{3,2,1,0:T(8,128)(2,1)S(1)}, bf16[1,1,128,1152]{3,2,1,0:T(8,128)(2,1)}, u32[]{:S(2)}) %copy-start.1) | copy-done | bytes 294936
  3.4 0.0 copy-start.2
  3.4 1.0 %copy-done.2 = bf16[36,3456]{1,0:T(8,128)(2,1)S(1)} copy-done((bf16[36,3456]{1,0:T(8,128)(2,1)S(1)}, bf16[36,3456]{1,0:T(8,128)(2,1)}, u32[]{:S(2)}) %copy-start.2) | copy-done | bytes 248856
  4.4 87.8 %shard_map.67 = (bf16[128,1152]{1,0:T(8,128)(2,1)S(1)}, bf16[128,3456]{1,0:T(8,128)(2,1)S(1)}, bf16[36,432]{1,0:T(8,128)(2,1)S(1)}) custom-call(s32[1]{0:T(128)S(6)} %copy.10.len_ref, bf16[128,3456]{1,0:T(8,128)(2,1)S(1)} %bitcast.5, bf16[36,3456]{1,0:T(8,128)(2,1)S(1)} %copy-done.2, bf16[128,1152]{1,0:T(8,128)(2,1)S(1)} %bitcast.7), custom_call_target="tpu_custom_call" | custom-call | tf_op jit(solution)/shard_map/pallas_call | solution.py:552
  92.2 0.7 copy.11
  92.9 0.9 copy.12
  93.8 0.6 copy.13
Async XLA Ops:
  1.3 1.2 %copy-start = (bf16[1,1,128,3456]{3,2,1,0:T(8,128)(2,1)S(1)}, bf16[1,1,128,3456]{3,2,1,0:T(8,128)(2,1)}, u32[]{:S(2)}) copy-start(bf16[1,1,128,3456]{3,2,1,0:T(8,128)(2,1)} %param.4) | copy-start | bytes 2654212
  2.4 1.0 %copy-start.1 = (bf16[1,1,128,1152]{3,2,1,0:T(8,128)(2,1)S(1)}, bf16[1,1,128,1152]{3,2,1,0:T(8,128)(2,1)}, u32[]{:S(2)}) copy-start(bf16[1,1,128,1152]{3,2,1,0:T(8,128)(2,1)} %param.7) | copy-start | bytes 884740
  3.4 1.0 %copy-start.2 = (bf16[36,3456]{1,0:T(8,128)(2,1)S(1)}, bf16[36,3456]{1,0:T(8,128)(2,1)}, u32[]{:S(2)}) copy-start(bf16[36,3456]{1,0:T(8,128)(2,1)} %w.1) | copy-start | bytes 746500

commit v3 on v2

--- a/solution.py
+++ b/solution.py
@@ -26,8 +26,8 @@
     return lax.dot_general(a, b, (((0,), (0,)), ((), ())), preferred_element_type=F32)
 
 
-def half(window, j):
-    return window[:, 0:256] if j < 2 else window[:, 128:384]
+def half(window, pair):
+    return window[:, 0:256] if pair == 0 else window[:, 128:384]
 
 
 def head_masks(off):
@@ -39,8 +39,17 @@
     return masks
 
 
+def two(window, pair, masks):
+    own = half(window, pair)
+    return jnp.concatenate([own * masks[2 * pair], own * masks[2 * pair + 1]], axis=0)
+
+
+def stack(array):
+    return jnp.concatenate([array[:, 0:128], array[:, 128:256]], axis=0)
+
+
 def join(parts):
-    left, right = parts[0] + parts[1], parts[2] + parts[3]
+    left, right = parts
     return jnp.concatenate(
         [left[:, 0:128], left[:, 128:256] + right[:, 0:128], right[:, 128:256]], axis=1
     )
@@ -48,29 +57,30 @@
 
 def forward4(q, k, v, masks, live):
     probs, outs = [], []
-    for j in range(4):
-        scores = dot_nt(half(q, j) * masks[j], half(k, j)) * SCALE
+    for pair in range(2):
+        scores = dot_nt(half(k, pair), two(q, pair, masks)) * SCALE
         if live is not None:
             scores = jnp.where(live, scores, -1e30)
-        expo = jnp.exp(scores - jnp.max(scores, axis=-1, keepdims=True))
-        prob = expo * (1.0 / jnp.sum(expo, axis=-1, keepdims=True))
+        expo = jnp.exp(scores - jnp.max(scores, axis=0, keepdims=True))
+        prob = expo * (1.0 / jnp.sum(expo, axis=0, keepdims=True))
         probs.append(prob)
-        outs.append(dot(prob.astype(BF16), half(v, j) * masks[j]))
+        outs.append(dot_tn(stack(prob.astype(BF16)), two(v, pair, masks)))
     return join(outs), probs
 
 
-def backward4(g, q, k, v, probs, masks):
+def backward4(g, q, k, v, probs, masks, values=True):
     dqs, dks, dvs = [], [], []
-    for j in range(4):
-        prob = probs[j]
-        gh = half(g, j) * masks[j]
-        dvs.append(dot_tn(prob.astype(BF16), gh))
-        gp = dot_nt(gh, half(v, j))
-        gs = prob * (gp - jnp.sum(gp * prob, axis=-1, keepdims=True))
+    for pair in range(2):
+        prob = probs[pair]
+        g_two = two(g, pair, masks)
+        if values:
+            dvs.append(dot(prob.astype(BF16), g_two))
+        gp = dot_nt(half(v, pair), g_two)
+        gs = prob * (gp - jnp.sum(gp * prob, axis=0, keepdims=True))
         low = (gs * SCALE).astype(BF16)
-        dqs.append(dot(low, half(k, j) * masks[j]))
-        dks.append(dot_tn(low, half(q, j) * masks[j]))
-    return join(dqs), join(dks), join(dvs)
+        dqs.append(dot_tn(stack(low), two(k, pair, masks)))
+        dks.append(dot(low, two(q, pair, masks)))
+    return (join(dqs), join(dks)) + ((join(dvs),) if values else ())
 
 
 def remote(src, dst, ssem, rsem, dp, s):
@@ -87,6 +97,10 @@
 Z_ORDER = (1, 7, 2, 6, 3, 5, 4)
 BLOCK = 144
 CHUNK = 384
+
+
+PART_AT = (2 * WIDTH, 0, WIDTH)
+OWNER = (0, 6, 1, 2, 3, 4, 5, 7)
 
 
 def placed(group, tile):
@@ -95,22 +109,22 @@
         low = max(128 * tile, 288 * part)
         high = min(128 * tile + 128, 288 * part + 288)
         if low < high:
-            shift = WIDTH * part + 288 * group - 288 * part
+            shift = PART_AT[part] + 288 * group - 288 * part
             found |= set(range((low + shift) // 432, (high - 1 + shift) // 432 + 1))
     return sorted(found)
 
 
 def tile_owner(tile):
-    return 2 * (tile % 4) + tile // 4
+    return 2 * (OWNER[tile] % 4) + OWNER[tile] // 4
 
 
 def kernel(
     len_ref, qkv_h, w, cot_h, bo, gqkv, gw,
-    qkv, cot, acc, prs, prt, blk, sob, wp, wr, wm, wf, so, cy, cz, c32, pj, to32, tob, ty, tf,
-    gp32, gpb, gs, gr, gz, gf, grad, pw, crv, kr, xr, zr, zb, fr, fs, fy, fd, gwf,
+    qkv, cot, acc, prs, prt, blk, sob, wp, wr, wm, wf, so, cy, cz, c32, pj, to32, tob, ty, tw, tf,
+    gp32, gpb, gs, gr, gz, gf, grad, pw, dv2, cre, kre, crv, kr, xr, zr, zb, fr, fs, fy, fd, gwf,
     in_s, wy_s, wy_r, wz_s, wz_r, wx_s, wx_r, wd_s, wd_r, cy_s, cy_r, cz_s, cz_r,
     sz_s, sz_r, sy_s, sy_r, ty_s, ty_r, tz_s, tz_r, gy_s, gy_r, gz_s, gz_r,
-    pc_s, pc_r, px_s, px_r, pz_s, pz_r, py_s, py_r, pd_s, pd_r,
+    pe_s, pe_r, pxe_s, pxe_r, pc_s, pc_r, px_s, px_r, pz_s, pz_r, py_s, py_r, pd_s, pd_r,
 ):
     dp, s = lax.axis_index("dp"), lax.axis_index("seq")
     y, z = lax.rem(s, NY), lax.div(s, NY)
@@ -153,43 +167,43 @@
     wrow = w[...].astype(F32)
     for g in range(NY):
         piece = jnp.concatenate(
-            [wrow[:, 288 * g + WIDTH * i: 288 * g + WIDTH * i + 288] for i in range(3)]
+            [wrow[:, 288 * g + at: 288 * g + at + 288] for at in PART_AT]
             + [jnp.zeros((36, 160), F32)], axis=1
         )
         piece = jnp.concatenate([piece, jnp.zeros((12, 1024), F32)], axis=0).astype(BF16)
         for t in range(8):
-            wp[g, t] = piece[:, 128 * t: 128 * t + 128]
+            wp[g, OWNER[t]] = piece[:, 128 * t: 128 * t + 128]
     wr[y] = wp[y, mine]
-    acc[...] = jnp.zeros_like(acc)
-    fd[...] = jnp.zeros_like(fd)
 
     def spatial_forward(group):
         at = pl.multiple_of(256 * group, 128)
         q, k, v = (qkv[:, pl.ds(at + WIDTH * i, 384)] for i in range(3))
         out, probs = forward4(q, k, v, head_masks(32 * group), None)
         acc[:, pl.ds(at, 384)] += out
-        for j in range(4):
-            prs[4 * group + j] = probs[j]
-
-    qkv_in.wait()
-    cot_in.wait()
-    spatial_forward(0)
-    cy[y] = cot[:, pl.ds(pl.multiple_of(256 * y, 128), 384)]
+        for j in range(2):
+            prs[2 * group + j] = probs[j]
+
 
     pl.semaphore_wait(barrier, NY + NZ + NX * NC - 3)
     for k in range(1, NY):
         to = at_y(k)
         send(wp.at[to, mine], wr.at[y], wy_s.at[k - 1], wy_r.at[k - 1], dp, z * NY + to)
+    acc[...] = jnp.zeros_like(acc)
+    fd[...] = jnp.zeros_like(fd)
+    cot_in.wait()
+    cy[y] = cot[:, pl.ds(pl.multiple_of(256 * y, 128), 384)]
     for k in range(1, NY):
         to = at_y(k)
         send(
             cot.at[:, pl.ds(pl.multiple_of(256 * to, 128), 384)], cy.at[y],
             cy_s.at[k - 1], cy_r.at[k - 1], dp, z * NY + to,
         )
-    spatial_forward(1)
-    spatial_forward(2)
-    spatial_forward(3)
+
+    qkv_in.wait()
+    for group in range(4):
+        spatial_forward(group)
     sob[...] = acc[:, 0:WIDTH].astype(BF16)
+    so[z, y] = sob[pl.ds(m16(16 * z), 16), :]
 
     for k in range(1, NY):
         arrived(wr.at[at_y(-k)], wy_s.at[k - 1], wy_r.at[k - 1])
@@ -210,9 +224,12 @@
             block = so.at[at_z(k), y]
             send(block, block, sy_s.at[order, i - 1], sy_r.at[order, i - 1], dp, z * NY + at_y(i))
 
-    for k in Z_ORDER:
-        block = wf.at[mine, rows(0)]
-        send(block, block, wz_s.at[k - 1], wz_r.at[k - 1], dp, at_z(k) * NY + y)
+    def weight_on(k, step, way):
+        block = wf.at[mine, rows(k)]
+        send(block, block, wz_s.at[way - 1], wz_r.at[way - 1], dp, at_z(step) * NY + y)
+
+    for k in (1, 7, 2, 6):
+        weight_on(0, k, k)
     weight_x(0, 0)
     for k in Z_ORDER:
         to = at_z(k)
@@ -220,10 +237,14 @@
             sob.at[pl.ds(m16(16 * to), 16)], so.at[z, y],
             sz_s.at[k - 1], sz_r.at[k - 1], dp, to * NY + y,
         )
-    so[z, y] = sob[pl.ds(m16(16 * z), 16), :]
     spread_y(0, 0)
     for order, k in enumerate(Z_ORDER):
         arrived(wf.at[mine, rows(-k)], wz_s.at[k - 1], wz_r.at[k - 1])
+        if k == 2:
+            weight_on(-2, 1, 3)
+            weight_on(-2, 2, 4)
+        if k == 6:
+            weight_on(2, -1, 5)
         weight_x(order + 1, -k)
         arrived(so.at[at_z(-k), y], sz_s.at[k - 1], sz_r.at[k - 1])
         spread_y(order + 1, -k)
@@ -254,15 +275,17 @@
     every = so[...].reshape(512, WIDTH)
     for t in range(4):
         if t < 3:
-            pair = dot(every, jnp.concatenate([wf[2 * t], wf[2 * t + 1]], axis=1))
+            pair = dot(
+                every, jnp.concatenate([wf[OWNER[2 * t]], wf[OWNER[2 * t + 1]]], axis=1)
+            )
             pj[2 * t], pj[2 * t + 1] = pair[:, 0:128], pair[:, 128:256]
         else:
-            pj[6] = dot(every, wf[6])
+            pj[6] = dot(every, wf[OWNER[6]])
 
     length = len_ref[0]
-    row = lax.broadcasted_iota(jnp.int32, (128, 128), 0)
-    col = lax.broadcasted_iota(jnp.int32, (128, 128), 1)
-    live = ((row >> 5) == (col >> 5)) & ((col & 31) < length)
+    key = lax.broadcasted_iota(jnp.int32, (128, 256), 0)
+    query = lax.broadcasted_iota(jnp.int32, (128, 256), 1) & 127
+    live = ((key >> 5) == (query >> 5)) & ((key & 31) < length)
     masks = head_masks(0)
 
     def rows_of(ref, first, b):
@@ -277,12 +300,12 @@
         )
 
     def temporal_forward(b, carry):
-        q = rows_of(pj, 0, b).astype(BF16)
-        k = pltpu.roll(rows_of(pj, 2, b), 384 - 32, 1).astype(BF16)
-        v = pltpu.roll(rows_of(pj, 4, b), 384 - 64, 1).astype(BF16)
+        v = rows_of(pj, 0, b).astype(BF16)
+        q = pltpu.roll(rows_of(pj, 2, b), 384 - 32, 1).astype(BF16)
+        k = pltpu.roll(rows_of(pj, 4, b), 384 - 64, 1).astype(BF16)
         blk[b, 0], blk[b, 1], blk[b, 2] = q, k, v
         out, probs = forward4(q, k, v, masks, live)
-        for j in range(4):
+        for j in range(2):
             prt[b, j] = probs[j]
         for i in range(4):
             for t in range(3):
@@ -291,7 +314,8 @@
                 ]
         return carry
 
-    lax.fori_loop(0, 4, temporal_forward, 0)
+    for b in range(0, 4):
+        temporal_forward(b, 0)
 
     t_out = jnp.concatenate([to32[t] for t in range(3)], axis=1)
     turned = t_out
@@ -312,35 +336,81 @@
     for t in range(3):
         c32[t] = turned[:, 128 * t: 128 * t + 128]
 
-    def temporal_backward(b, carry):
-        q, k, v = blk[b, 0], blk[b, 1], blk[b, 2]
-        g = rows_of(c32, 0, b).astype(BF16)
-        dq, dk, dv = backward4(g, q, k, v, [prt[b, j] for j in range(4)], masks)
-        dk, dv = pltpu.roll(dk, 32, 1), pltpu.roll(dv, 64, 1)
-        packed = jnp.concatenate(
-            [dq[:, 0:256], dq[:, 256:384] + dk[:, 0:128], dk[:, 128:256],
-             dk[:, 256:384] + dv[:, 0:128], dv[:, 128:384]], axis=1
-        )
+    def scatter(ref, first, b, array):
         for i in range(4):
-            for t in range(7):
-                gp32[t, pl.ds(4 * b + i, 32, stride=16), :] = packed[
+            for t in range(array.shape[1] // 128):
+                ref[first + t, pl.ds(4 * b + i, 32, stride=16), :] = array[
                     32 * i: 32 * i + 32, 128 * t: 128 * t + 128
                 ]
+
+    def temporal_values(b, carry):
+        g = rows_of(c32, 0, b).astype(BF16)
+        blk[b, 3] = g
+        dv = join([
+            dot(prt[b, pair].astype(BF16), two(g, pair, masks)) for pair in range(2)
+        ])
+        scatter(gp32, 0, b, dv[:, 0:256])
+        dv2[b] = dv[:, 256:384]
         return carry
 
-    lax.fori_loop(0, 4, temporal_backward, 0)
-
-    for t in range(7):
+    def temporal_backward(b, carry):
+        q, k, v, g = blk[b, 0], blk[b, 1], blk[b, 2], blk[b, 3]
+        dq, dk = backward4(g, q, k, v, [prt[b, j] for j in range(2)], masks, False)
+        dq, dk = pltpu.roll(dq, 32, 1), pltpu.roll(dk, 64, 1)
+        packed = jnp.concatenate(
+            [dv2[b] + dq[:, 0:128], dq[:, 128:256], dq[:, 256:384] + dk[:, 0:128], dk[:, 128:384]],
+            axis=1,
+        )
+        scatter(gp32, 2, b, packed)
+        return carry
+
+    def weight_part(at, low, high):
+        part = dot_tn(
+            so[:, :, :, at: at + CHUNK].reshape(512, CHUNK), gpb[:, 128 * low: 128 * high]
+        ).astype(BF16)
+        for t in range(low, high):
+            pw[OWNER[t], at: at + CHUNK] = part[:, 128 * (t - low): 128 * (t - low) + 128]
+
+    early, late = x == 2 * c, (x != 2 * c) & (mine != 7)
+
+    def early_weight():
+        for i in range(3):
+            weight_part(CHUNK * i, 0, 2)
+        send(pw.at[6 - 6 * c], cre, pe_s, pe_r, sib, s)
+
+    def early_to():
+        k = lax.rem(2 * c - x + NX, NX)
+        slot = jnp.maximum(k - 1, 0)
+        return remote(
+            kre, xr.at[slot], pxe_s, pxe_r.at[slot], 2 * c * NC + c, s
+        )
+
+    def early_sum():
+        arrived(cre, pe_s, pe_r)
+        kre[...] = (pw[6 * c].astype(F32) + cre[...].astype(F32)).astype(BF16)
+
+        @pl.when(x != 2 * c)
+        def _():
+            early_to().start()
+
+    for b in range(0, 4):
+        temporal_values(b, 0)
+    for t in range(2):
         gpb[:, 128 * t: 128 * t + 128] = gp32[t].astype(BF16)
-    gpb[:, 896:1024] = jnp.zeros((512, 128), BF16)
+    early_weight()
+    for b in range(0, 2):
+        temporal_backward(b, 0)
+    early_sum()
+    for b in range(2, 4):
+        temporal_backward(b, 0)
+    for t in range(2, 7):
+        gpb[:, 128 * t: 128 * t + 128] = gp32[t].astype(BF16)
 
     def weight_chunk(i):
         at = CHUNK * i
-        part = dot_tn(so[:, :, :, at: at + CHUNK].reshape(512, CHUNK), gpb[...]).astype(BF16)
-        for t in range(8):
-            pw[t, at: at + CHUNK] = part[:, 128 * t: 128 * t + 128]
+        weight_part(at, 2, 7)
         send(
-            pw.at[pl.ds(4 - 4 * c, 4), at: at + CHUNK], crv.at[:, at: at + CHUNK],
+            pw.at[pl.ds(4 - 3 * c, 3), at: at + CHUNK], crv.at[:, at: at + CHUNK],
             pc_s.at[i], pc_r.at[i], sib, s,
         )
 
@@ -350,11 +420,12 @@
         for t in range(4):
             if t < 3:
                 weight = jnp.concatenate(
-                    [wf[2 * t, at: at + CHUNK], wf[2 * t + 1, at: at + CHUNK]], axis=1
+                    [wf[OWNER[2 * t], at: at + CHUNK], wf[OWNER[2 * t + 1], at: at + CHUNK]],
+                    axis=1,
                 )
                 part = part + dot_nt(gpb[:, 256 * t: 256 * t + 256], weight)
             else:
-                part = part + dot_nt(gpb[:, 768:896], wf[6, at: at + CHUNK])
+                part = part + dot_nt(gpb[:, 768:896], wf[OWNER[6], at: at + CHUNK])
         gs[i] = part.astype(BF16).reshape(NZ, NY, 16, CHUNK)
         for k in range(1, NY):
             to = at_y(k)
@@ -363,26 +434,47 @@
                 gy_s.at[i, k - 1], gy_r.at[i, k - 1], dp, z * NY + to,
             )
 
+    def late_to(i, k):
+        at = CHUNK * i
+        to = at_x(k)
+        wanted = (to != 2 * c) & (4 * c + to != 7)
+        return wanted, remote(
+            kr.at[jnp.clip(to - 1 + c, 0, 2), at: at + CHUNK], xr.at[k - 1, at: at + CHUNK],
+            px_s.at[i, k - 1], px_r.at[i, k - 1], to * NC + c, s,
+        )
+
     def weight_sum(i):
         at = CHUNK * i
         arrived(crv.at[:, at: at + CHUNK], pc_s.at[i], pc_r.at[i])
         kr[:, at: at + CHUNK] = (
-            pw[pl.ds(4 * c, 4), at: at + CHUNK].astype(F32) + crv[:, at: at + CHUNK].astype(F32)
+            pw[pl.ds(1 + 3 * c, 3), at: at + CHUNK].astype(F32)
+            + crv[:, at: at + CHUNK].astype(F32)
         ).astype(BF16)
         for k in range(1, NX):
-            to = at_x(k)
-            send(
-                kr.at[to, at: at + CHUNK], xr.at[k - 1, at: at + CHUNK],
-                px_s.at[i, k - 1], px_r.at[i, k - 1], to * NC + c, s,
-            )
+            wanted, copy = late_to(i, k)
+            pl.when(wanted)(copy.start)
 
     def weight_z(i, blocks):
         at = CHUNK * i
-        for k in range(1, NX):
-            arrived(xr.at[k - 1, at: at + CHUNK], px_s.at[i, k - 1], px_r.at[i, k - 1])
-        total = kr[x, at: at + CHUNK].astype(F32)
+
+        @pl.when(late)
+        def _():
+            for k in range(1, NX):
+                arrived(xr.at[k - 1, at: at + CHUNK], px_s.at[i, k - 1], px_r.at[i, k - 1])
+
+        if i == 0:
+            @pl.when(early)
+            def _():
+                for k in range(1, NX):
+                    arrived(xr.at[k - 1], pxe_s, pxe_r.at[k - 1])
+
+        total = jnp.where(
+            early, kre[at: at + CHUNK].astype(F32),
+            kr[jnp.clip(x - 1 + c, 0, 2), at: at + CHUNK].astype(F32),
+        )
         for k in range(1, NX):
             total = total + xr[k - 1, at: at + CHUNK].astype(F32)
+        total = jnp.where(early | late, total, 0.0)
         zr[at: at + CHUNK] = total.astype(BF16)
         for b in blocks:
             @pl.when(z != b)
@@ -417,10 +509,64 @@
     def spatial_backward(group):
         at = 256 * group
         q, k, v = (qkv[:, at + WIDTH * i: at + WIDTH * i + 384] for i in range(3))
-        probs = [prs[4 * group + j] for j in range(4)]
+        probs = [prs[2 * group + j] for j in range(2)]
         grads = backward4(grad[:, at: at + 384], q, k, v, probs, head_masks(32 * group))
         for i in range(3):
             acc[:, at + WIDTH * i: at + WIDTH * i + 384] += grads[i]
+
+    def out_z():
+        for k in range(1, NY):
+            arrived(ty.at[at_y(-k)], ty_s.at[k - 1], ty_r.at[k - 1])
+        whole = [None] * 9
+        for i in range(NY):
+            for t in range(3):
+                tile = ty[i, :, :, 128 * t: 128 * t + 128].astype(F32)
+                at = 2 * i + t
+                whole[at] = tile if whole[at] is None else whole[at] + tile
+        for t in range(9):
+            tw[:, :, 128 * t: 128 * t + 128] = whole[t].astype(BF16)
+        for k in Z_ORDER:
+            to = at_z(k)
+            send(tw.at[to], tf.at[z], tz_s.at[k - 1], tz_r.at[k - 1], dp, to * NY + y)
+        tf[z] = tw[z]
+
+    def final_y():
+        zb[z] = zr[pl.ds(m16(BLOCK * z), BLOCK)]
+        for b in range(NZ):
+            @pl.when(z != b)
+            def _():
+                arrived(zb.at[b], pz_s.at[b], pz_r.at[b])
+        total = zb[0].astype(F32)
+        for i in range(1, NZ):
+            total = total + zb[i].astype(F32)
+        fr[0:BLOCK, :] = total
+        fr[BLOCK:160, :] = jnp.zeros((16, 128), F32)
+        for i in range(NY):
+            fs[i] = fr[36 * i: 36 * i + 48, :].astype(BF16)
+        for k in range(1, NY):
+            to = at_y(k)
+            send(fs.at[to], fy.at[y], py_s.at[k - 1], py_r.at[k - 1], dp, z * NY + to)
+        fy[y] = fs[y]
+
+    def moves(tile):
+        return [
+            (g, d) for g in range(NY) for d in placed(g, tile) if d != tile_owner(tile)
+        ]
+
+    def move(tile, g, d):
+        return remote(
+            fy.at[g], fd.at[OWNER[tile], g], pd_s.at[g, d], pd_r.at[tile, g], d, s
+        )
+
+    def final_dp():
+        for k in range(1, NY):
+            arrived(fy.at[at_y(-k)], py_s.at[k - 1], py_r.at[k - 1])
+        for tile in range(7):
+            @pl.when(dp == tile_owner(tile))
+            def _():
+                for g, d in moves(tile):
+                    move(tile, g, d).start()
+        fd[mine] = fy[...]
 
     weight_chunk(0)
     back_chunk(0)
@@ -429,93 +575,50 @@
     weight_chunk(2)
     weight_sum(1)
     back_chunk(1)
+    weight_sum(2)
     back_chunk(2)
-    weight_sum(2)
-
-    for k in range(1, NY):
-        arrived(ty.at[at_y(-k)], ty_s.at[k - 1], ty_r.at[k - 1])
-    for k in Z_ORDER:
-        to = at_z(k)
-        send(ty.at[:, to], tf.at[z], tz_s.at[k - 1], tz_r.at[k - 1], dp, to * NY + y)
-    tf[z] = ty[:, z]
+    out_z()
     acc[...] = jnp.zeros_like(acc)
-
+    weight_z(0, (0, 1))
     back_sum(0)
-    weight_z(0, (0, 1))
+    weight_z(1, (2, 3, 4))
     back_sum(1)
-    weight_z(1, (2, 3, 4))
+    weight_z(2, (5, 6, 7))
     back_sum(2)
     back_done(0)
     spatial_backward(0)
-    weight_z(2, (5, 6, 7))
+    final_y()
     back_done(1)
     spatial_backward(1)
+    final_dp()
     back_done(2)
     spatial_backward(2)
     spatial_backward(3)
-
-    zb[z] = zr[pl.ds(m16(BLOCK * z), BLOCK)]
-    for b in range(NZ):
-        @pl.when(z != b)
-        def _():
-            arrived(zb.at[b], pz_s.at[b], pz_r.at[b])
-    total = zb[0].astype(F32)
-    for i in range(1, NZ):
-        total = total + zb[i].astype(F32)
-    fr[0:BLOCK, :] = total
-    fr[BLOCK:160, :] = jnp.zeros((16, 128), F32)
-    for i in range(NY):
-        fs[i] = fr[36 * i: 36 * i + 48, :].astype(BF16)
-    for k in range(1, NY):
-        to = at_y(k)
-        send(fs.at[to], fy.at[y], py_s.at[k - 1], py_r.at[k - 1], dp, z * NY + to)
-    fy[y] = fs[y]
-
     gqkv[...] = acc[...].astype(BF16)
     for k in Z_ORDER:
         arrived(tf.at[at_z(-k)], tz_s.at[k - 1], tz_r.at[k - 1])
-    acc[:, 0:WIDTH] = sob[...].astype(F32)
-    for i in range(NY):
-        acc[:, 256 * i: 256 * i + 384] += tf[:, i].reshape(128, 384).astype(F32)
-    bo[...] = acc[:, 0:WIDTH].astype(BF16)
-
-    for k in range(1, NY):
-        arrived(fy.at[at_y(-k)], py_s.at[k - 1], py_r.at[k - 1])
-
-    def moves(tile):
-        return [
-            (g, d) for g in range(NY) for d in placed(g, tile) if d != tile_owner(tile)
-        ]
-
-    def move(tile, g, d):
-        return remote(fy.at[g], fd.at[tile, g], pd_s.at[g, d], pd_r.at[tile, g], d, s)
-
-    for tile in range(7):
-        @pl.when(dp == tile_owner(tile))
-        def _():
-            for g, d in moves(tile):
-                move(tile, g, d).start()
-    fd[mine] = fy[...]
+    bo[...] = (sob[...].astype(F32) + tf[...].reshape(128, WIDTH).astype(F32)).astype(BF16)
+
     for d in range(NX * NC):
         @pl.when(dp == d)
         def _():
             for tile in range(7):
                 for g, to in moves(tile):
                     if to == d:
-                        arrived(fd.at[tile, g], pd_s.at[g, d], pd_r.at[tile, g])
+                        arrived(fd.at[OWNER[tile], g], pd_s.at[g, d], pd_r.at[tile, g])
     gwf[...] = jnp.zeros_like(gwf)
     lane = lax.broadcasted_iota(jnp.int32, (48, 384), 1)
     for g in range(NY):
         for i in range(3):
             window = jnp.concatenate(
-                [fd[2 * i + t, g].astype(F32) for t in range(3)], axis=1
+                [fd[OWNER[2 * i + t], g].astype(F32) for t in range(3)], axis=1
             )
             if i > 0:
                 window = pltpu.roll(window, 384 - 32 * i, 1)
             window = jnp.where(lane < 288, window, 0.0)
             if g > 0:
                 window = pltpu.roll(window, 32 * g, 1)
-            at = WIDTH * i + 256 * g
+            at = PART_AT[i] + 256 * g
             gwf[:, at: at + 384] += window
     picked = jnp.zeros((48, 432), F32)
     for d in range(NX * NC):
@@ -524,6 +627,15 @@
 
     for copy in sent:
         copy.wait_send()
+
+    @pl.when(x != 2 * c)
+    def _():
+        early_to().wait_send()
+
+    for i in range(3):
+        for k in range(1, NX):
+            wanted, copy = late_to(i, k)
+            pl.when(wanted)(copy.wait_send)
     for b in range(NZ):
         @pl.when(z != b)
         def _():
@@ -540,7 +652,7 @@
 def local(spatial_qkv, lengths, w_qkv, cotangent):
     frames, patches = spatial_qkv.shape[1], spatial_qkv.shape[2]
     vmem = pl.BlockSpec(memory_space=pltpu.VMEM)
-    anywhere = pl.BlockSpec(memory_space=pltpu.HBM)
+    hbm = pl.BlockSpec(memory_space=pltpu.HBM)
     dma = pltpu.SemaphoreType.DMA
 
     def bf(*shape):
@@ -556,15 +668,15 @@
             jax.ShapeDtypeStruct((patches, 3 * WIDTH), BF16),
             jax.ShapeDtypeStruct((36, 432), BF16),
         ),
-        in_specs=[pl.BlockSpec(memory_space=pltpu.SMEM), anywhere, vmem, anywhere],
+        in_specs=[pl.BlockSpec(memory_space=pltpu.SMEM), hbm, vmem, hbm],
         out_specs=(vmem, vmem, vmem),
         scratch_shapes=[
             bf(128, 3 * WIDTH),
             bf(128, WIDTH),
             fl(128, 3 * WIDTH),
-            fl(16, 128, 128),
-            fl(4, 4, 128, 128),
-            bf(4, 3, 128, 384),
+            fl(8, 128, 256),
+            fl(4, 2, 128, 256),
+            bf(4, 4, 128, 384),
             bf(128, WIDTH),
             bf(4, 8, 48, 128),
             bf(4, 48, 128),
@@ -578,7 +690,8 @@
             fl(3, 512, 128),
             bf(8, 4, 16, 384),
             bf(4, 8, 16, 384),
-            bf(8, 4, 16, 384),
+            bf(8, 16, WIDTH),
+            bf(8, 16, WIDTH),
             fl(7, 512, 128),
             bf(512, 1024),
             bf(3, 8, 4, 16, CHUNK),
@@ -587,8 +700,11 @@
             bf(3, 8, 16, CHUNK),
             bf(128, WIDTH),
             bf(8, WIDTH, 128),
-            bf(4, WIDTH, 128),
-            bf(4, WIDTH, 128),
+            fl(4, 128, 128),
+            bf(WIDTH, 128),
+            bf(WIDTH, 128),
+            bf(3, WIDTH, 128),
+            bf(3, WIDTH, 128),
             bf(3, WIDTH, 128),
             bf(WIDTH, 128),
             bf(8, BLOCK, 128),
@@ -603,11 +719,12 @@
             dma((7,)), dma((7,)), dma((8, 3)), dma((8, 3)),
             dma((3,)), dma((3,)), dma((7,)), dma((7,)),
             dma((3, 3)), dma((3, 3)), dma((3, 7)), dma((3, 7)),
+            dma, dma, dma, dma((3,)),
             dma((3,)), dma((3,)), dma((3, 3)), dma((3, 3)), dma((8,)), dma((8,)),
             dma((3,)), dma((3,)), dma((4, 8)), dma((8, 4)),
         ],
         compiler_params=pltpu.CompilerParams(
-            collective_id=0, has_side_effects=True, vmem_limit_bytes=50 * 1024 * 1024
+            collective_id=0, has_side_effects=True, vmem_limit_bytes=52 * 1024 * 1024
         ),
     )(
         lengths, spatial_qkv.reshape(patches, 3 * WIDTH), w_qkv,

time: 94.6 us -> 83.9 us (0.89)
  Pallas kernels: 87.8 us -> 78.3 us
  local copies, waits for them, and re-layouts: 5.32 us -> 4.15 us
    pallas_call x1, Pallas kernels: 87.8 us -> 78.3 us  [local(): pl.pallas_call(kernel, out_shape=(jax.ShapeDtypeStruct((patches, WIDTH),...]
    unnamed x9 -> x7, local copies, waits for them, and re-layouts: 5.32 us -> 4.15 us
where the time goes in v3:
time: 83.9 us; the launch traced here: 83.7 us
  Pallas kernels  78.3 us (93%)
  local copies, waits for them, and re-layouts  4.15 us (5%)
  between operations  1.3 us (2%)
    pallas_call x1, Pallas kernels, local(): pl.pallas_call(kernel, out_shape=(jax.ShapeDtypeStruct((patches, WIDTH),...  78.3 us
    unnamed x7, local copies, waits for them, and re-layouts  4.15 us

profile of v3, /device:TPU:1, one launch (start us, length us, event | category | flops | bytes accessed | tf_op | source)
XLA Modules:
  0.0 83.7 jit_solution(4074203031906087390)
XLA Ops:
  1.3 0.0 copy-start
  1.3 1.0 %copy-done = bf16[1,1,128,1152]{3,2,1,0:T(8,128)(2,1)S(1)} copy-done((bf16[1,1,128,1152]{3,2,1,0:T(8,128)(2,1)S(1)}, bf16[1,1,128,1152]{3,2,1,0:T(8,128)(2,1)}, u32[]{:S(2)}) %copy-start) | copy-done | bytes 294936
  2.2 0.0 copy-start.1
  2.2 1.0 %copy-done.1 = bf16[36,3456]{1,0:T(8,128)(2,1)S(1)} copy-done((bf16[36,3456]{1,0:T(8,128)(2,1)S(1)}, bf16[36,3456]{1,0:T(8,128)(2,1)}, u32[]{:S(2)}) %copy-start.1) | copy-done | bytes 248856
  3.2 78.3 %shard_map.67 = (bf16[128,1152]{1,0:T(8,128)(2,1)S(1)}, bf16[128,3456]{1,0:T(8,128)(2,1)S(1)}, bf16[36,432]{1,0:T(8,128)(2,1)S(1)}) custom-call(s32[1]{0:T(128)S(6)} %copy.10.len_ref, bf16[128,3456]{1,0:T(8,128)(2,1)} %bitcast.7, bf16[36,3456]{1,0:T(8,128)(2,1)S(1)} %copy-done.1, bf16[128,1152]{1,0:T(8,128)(2,1)S(1)} %bitcast.6), custom_call_target="tpu_custom_call" | custom-call | tf_op jit(solution)/shard_map/pallas_call | solution.py:664
  81.5 0.7 copy.11
  82.2 0.9 %copy.12 = bf16[1,1,128,3456]{3,2,1,0:T(8,128)(2,1)} copy(bf16[1,1,128,3456]{3,2,1,0:T(8,128)(2,1)S(1)} %bitcast.4) | data formatting | bytes 1769472
  83.1 0.6 copy.13
Async XLA Ops:
  1.3 1.0 %copy-start = (bf16[1,1,128,1152]{3,2,1,0:T(8,128)(2,1)S(1)}, bf16[1,1,128,1152]{3,2,1,0:T(8,128)(2,1)}, u32[]{:S(2)}) copy-start(bf16[1,1,128,1152]{3,2,1,0:T(8,128)(2,1)} %param.7) | copy-start | bytes 884740
  2.2 1.0 %copy-start.1 = (bf16[36,3456]{1,0:T(8,128)(2,1)S(1)}, bf16[36,3456]{1,0:T(8,128)(2,1)}, u32[]{:S(2)}) copy-start(bf16[36,3456]{1,0:T(8,128)(2,1)} %w.1) | copy-start | bytes 746500

commit v4 on v3

--- a/solution.py
+++ b/solution.py
@@ -572,12 +572,12 @@
     back_chunk(0)
     weight_chunk(1)
     weight_sum(0)
+    out_z()
     weight_chunk(2)
     weight_sum(1)
     back_chunk(1)
     weight_sum(2)
     back_chunk(2)
-    out_z()
     acc[...] = jnp.zeros_like(acc)
     weight_z(0, (0, 1))
     back_sum(0)

time: 83.9 us -> 81.6 us (0.973)
  Pallas kernels: 78.3 us -> 75.6 us
    pallas_call x1, Pallas kernels: 78.3 us -> 75.6 us  [local(): pl.pallas_call(kernel, out_shape=(jax.ShapeDtypeStruct((patches, WIDTH),...]
where the time goes in v4:
time: 81.6 us; the launch traced here: 81 us
  Pallas kernels  75.6 us (93%)
  local copies, waits for them, and re-layouts  4.15 us (5%)
  between operations  1.3 us (2%)
    pallas_call x1, Pallas kernels, local(): pl.pallas_call(kernel, out_shape=(jax.ShapeDtypeStruct((patches, WIDTH),...  75.6 us
    unnamed x7, local copies, waits for them, and re-layouts  4.15 us

profile of v4, /device:TPU:1, one launch (start us, length us, event | category | flops | bytes accessed | tf_op | source)
XLA Modules:
  0.0 81.0 jit_solution(6288370037504531318)
XLA Ops:
  1.3 0.0 copy-start
  1.3 1.0 %copy-done = bf16[1,1,128,1152]{3,2,1,0:T(8,128)(2,1)S(1)} copy-done((bf16[1,1,128,1152]{3,2,1,0:T(8,128)(2,1)S(1)}, bf16[1,1,128,1152]{3,2,1,0:T(8,128)(2,1)}, u32[]{:S(2)}) %copy-start) | copy-done | bytes 294936
  2.2 0.0 copy-start.1
  2.2 1.0 %copy-done.1 = bf16[36,3456]{1,0:T(8,128)(2,1)S(1)} copy-done((bf16[36,3456]{1,0:T(8,128)(2,1)S(1)}, bf16[36,3456]{1,0:T(8,128)(2,1)}, u32[]{:S(2)}) %copy-start.1) | copy-done | bytes 248856
  3.2 75.6 %shard_map.67 = (bf16[128,1152]{1,0:T(8,128)(2,1)S(1)}, bf16[128,3456]{1,0:T(8,128)(2,1)S(1)}, bf16[36,432]{1,0:T(8,128)(2,1)S(1)}) custom-call(s32[1]{0:T(128)S(6)} %copy.10.len_ref, bf16[128,3456]{1,0:T(8,128)(2,1)} %bitcast.7, bf16[36,3456]{1,0:T(8,128)(2,1)S(1)} %copy-done.1, bf16[128,1152]{1,0:T(8,128)(2,1)S(1)} %bitcast.6), custom_call_target="tpu_custom_call" | custom-call | tf_op jit(solution)/shard_map/pallas_call | solution.py:664
  78.8 0.7 copy.11
  79.5 0.9 %copy.12 = bf16[1,1,128,3456]{3,2,1,0:T(8,128)(2,1)} copy(bf16[1,1,128,3456]{3,2,1,0:T(8,128)(2,1)S(1)} %bitcast.4) | data formatting | bytes 1769472
  80.4 0.6 copy.13
Async XLA Ops:
  1.3 1.0 %copy-start = (bf16[1,1,128,1152]{3,2,1,0:T(8,128)(2,1)S(1)}, bf16[1,1,128,1152]{3,2,1,0:T(8,128)(2,1)}, u32[]{:S(2)}) copy-start(bf16[1,1,128,1152]{3,2,1,0:T(8,128)(2,1)} %param.7) | copy-start | bytes 884740
  2.2 1.0 %copy-start.1 = (bf16[36,3456]{1,0:T(8,128)(2,1)S(1)}, bf16[36,3456]{1,0:T(8,128)(2,1)}, u32[]{:S(2)}) copy-start(bf16[36,3456]{1,0:T(8,128)(2,1)} %w.1) | copy-start | bytes 746500

commit v5 on v4

--- a/solution.py
+++ b/solution.py
@@ -121,10 +121,10 @@
 def kernel(
     len_ref, qkv_h, w, cot_h, bo, gqkv, gw,
     qkv, cot, acc, prs, prt, blk, sob, wp, wr, wm, wf, so, cy, cz, c32, pj, to32, tob, ty, tw, tf,
-    gp32, gpb, gs, gr, gz, gf, grad, pw, dv2, cre, kre, crv, kr, xr, zr, zb, fr, fs, fy, fd, gwf,
+    gp32, gpb, gs, gr, gz, gf, grad, pw, dv2, cre, kre, crv, kr, xr, zr, zb, fr, fs, fd, gwf,
     in_s, wy_s, wy_r, wz_s, wz_r, wx_s, wx_r, wd_s, wd_r, cy_s, cy_r, cz_s, cz_r,
     sz_s, sz_r, sy_s, sy_r, ty_s, ty_r, tz_s, tz_r, gy_s, gy_r, gz_s, gz_r,
-    pe_s, pe_r, pxe_s, pxe_r, pc_s, pc_r, px_s, px_r, pz_s, pz_r, py_s, py_r, pd_s, pd_r,
+    pe_s, pe_r, pxe_s, pxe_r, pc_s, pc_r, px_s, px_r, pz_s, pz_r, pd_s, pd_r,
 ):
     dp, s = lax.axis_index("dp"), lax.axis_index("seq")
     y, z = lax.rem(s, NY), lax.div(s, NY)
@@ -151,14 +151,11 @@
         remote(dst, dst, ssem, rsem, dp, s).wait_recv()
 
     barrier = pltpu.get_barrier_semaphore()
-    for k in range(1, NY):
-        pl.semaphore_signal(barrier, inc=1, device_id=(dp, z * NY + at_y(k)), device_id_type=MESH)
     for k in range(1, NZ):
         pl.semaphore_signal(barrier, inc=1, device_id=(dp, at_z(k) * NY + y), device_id_type=MESH)
-    for k in range(1, NX * NC):
-        pl.semaphore_signal(
-            barrier, inc=1, device_id=(lax.rem(dp + k, NX * NC), s), device_id_type=MESH
-        )
+    for k in range(1, NX * NC * NY):
+        to = (lax.rem(dp + k, NX * NC), z * NY + at_y(k // (NX * NC)))
+        pl.semaphore_signal(barrier, inc=1, device_id=to, device_id_type=MESH)
     qkv_in = pltpu.make_async_copy(qkv_h, qkv, in_s.at[0])
     cot_in = pltpu.make_async_copy(cot_h, cot, in_s.at[1])
     qkv_in.start()
@@ -184,7 +181,7 @@
             prs[2 * group + j] = probs[j]
 
 
-    pl.semaphore_wait(barrier, NY + NZ + NX * NC - 3)
+    pl.semaphore_wait(barrier, NZ + NX * NC * NY - 2)
     for k in range(1, NY):
         to = at_y(k)
         send(wp.at[to, mine], wr.at[y], wy_s.at[k - 1], wy_r.at[k - 1], dp, z * NY + to)
@@ -543,30 +540,20 @@
         fr[BLOCK:160, :] = jnp.zeros((16, 128), F32)
         for i in range(NY):
             fs[i] = fr[36 * i: 36 * i + 48, :].astype(BF16)
-        for k in range(1, NY):
-            to = at_y(k)
-            send(fs.at[to], fy.at[y], py_s.at[k - 1], py_r.at[k - 1], dp, z * NY + to)
-        fy[y] = fs[y]
-
-    def moves(tile):
-        return [
-            (g, d) for g in range(NY) for d in placed(g, tile) if d != tile_owner(tile)
-        ]
-
-    def move(tile, g, d):
-        return remote(
-            fy.at[g], fd.at[OWNER[tile], g], pd_s.at[g, d], pd_r.at[tile, g], d, s
-        )
-
-    def final_dp():
-        for k in range(1, NY):
-            arrived(fy.at[at_y(-k)], py_s.at[k - 1], py_r.at[k - 1])
+        each_move(lambda copy: copy.start())
+        fd[mine, y] = fs[y]
+
+    def each_move(act):
         for tile in range(7):
-            @pl.when(dp == tile_owner(tile))
-            def _():
-                for g, d in moves(tile):
-                    move(tile, g, d).start()
-        fd[mine] = fy[...]
+            for g in range(NY):
+                @pl.when((mine == OWNER[tile]) & (y == g))
+                def _():
+                    for d in placed(g, tile):
+                        for k in range(1 if d == tile_owner(tile) else 0, NY):
+                            act(remote(
+                                fs.at[at_y(k)], fd.at[OWNER[tile], g],
+                                pd_s.at[k, d], pd_r.at[tile, g], d, z * NY + at_y(k),
+                            ))
 
     weight_chunk(0)
     back_chunk(0)
@@ -590,7 +577,6 @@
     final_y()
     back_done(1)
     spatial_backward(1)
-    final_dp()
     back_done(2)
     spatial_backward(2)
     spatial_backward(3)
@@ -603,9 +589,17 @@
         @pl.when(dp == d)
         def _():
             for tile in range(7):
-                for g, to in moves(tile):
-                    if to == d:
-                        arrived(fd.at[OWNER[tile], g], pd_s.at[g, d], pd_r.at[tile, g])
+                for g in range(NY):
+                    if d not in placed(g, tile):
+                        continue
+                    copy = remote(
+                        fd.at[OWNER[tile], g], fd.at[OWNER[tile], g],
+                        pd_s.at[0, d], pd_r.at[tile, g], d, s,
+                    )
+                    if d == tile_owner(tile):
+                        pl.when(y != g)(copy.wait_recv)
+                    else:
+                        copy.wait_recv()
     gwf[...] = jnp.zeros_like(gwf)
     lane = lax.broadcasted_iota(jnp.int32, (48, 384), 1)
     for g in range(NY):
@@ -642,11 +636,7 @@
             remote(
                 zr.at[BLOCK * b: BLOCK * b + BLOCK], zb.at[z], pz_s.at[b], pz_r.at[z], dp, s
             ).wait_send()
-    for tile in range(7):
-        @pl.when(dp == tile_owner(tile))
-        def _():
-            for g, d in moves(tile):
-                move(tile, g, d).wait_send()
+    each_move(lambda copy: copy.wait_send())
 
 
 def local(spatial_qkv, lengths, w_qkv, cotangent):
@@ -710,7 +700,6 @@
             bf(8, BLOCK, 128),
             fl(160, 128),
             bf(4, 48, 128),
-            bf(4, 48, 128),
             bf(8, 4, 48, 128),
             fl(48, 3 * WIDTH),
             dma((2,)), dma((3,)), dma((3,)), dma((7,)), dma((7,)),
@@ -721,7 +710,7 @@
             dma((3, 3)), dma((3, 3)), dma((3, 7)), dma((3, 7)),
             dma, dma, dma, dma((3,)),
             dma((3,)), dma((3,)), dma((3, 3)), dma((3, 3)), dma((8,)), dma((8,)),
-            dma((3,)), dma((3,)), dma((4, 8)), dma((8, 4)),
+            dma((4, 8)), dma((8, 4)),
         ],
         compiler_params=pltpu.CompilerParams(
             collective_id=0, has_side_effects=True, vmem_limit_bytes=52 * 1024 * 1024

time: 81.6 us -> 81 us (level)
  the two profiles are of different devices: /device:TPU:1 before, /device:TPU:26 now
where the time goes in v5:
time: 81 us; the launch traced here: 80.8 us
  Pallas kernels  75.4 us (93%)
  local copies, waits for them, and re-layouts  4.15 us (5%)
  between operations  1.3 us (2%)
    pallas_call x1, Pallas kernels, local(): pl.pallas_call(kernel, out_shape=(jax.ShapeDtypeStruct((patches, WIDTH),...  75.4 us
    unnamed x7, local copies, waits for them, and re-layouts  4.15 us

profile of v5, /device:TPU:26, one launch (start us, length us, event | category | flops | bytes accessed | tf_op | source)
XLA Modules:
  0.0 80.8 jit_solution(922710352318377644)
XLA Ops:
  1.3 0.0 copy-start
  1.3 1.0 %copy-done = bf16[1,1,128,1152]{3,2,1,0:T(8,128)(2,1)S(1)} copy-done((bf16[1,1,128,1152]{3,2,1,0:T(8,128)(2,1)S(1)}, bf16[1,1,128,1152]{3,2,1,0:T(8,128)(2,1)}, u32[]{:S(2)}) %copy-start) | copy-done | bytes 294936
  2.2 0.0 copy-start.1
  2.2 1.0 %copy-done.1 = bf16[36,3456]{1,0:T(8,128)(2,1)S(1)} copy-done((bf16[36,3456]{1,0:T(8,128)(2,1)S(1)}, bf16[36,3456]{1,0:T(8,128)(2,1)}, u32[]{:S(2)}) %copy-start.1) | copy-done | bytes 248856
  3.2 75.4 %shard_map.67 = (bf16[128,1152]{1,0:T(8,128)(2,1)S(1)}, bf16[128,3456]{1,0:T(8,128)(2,1)S(1)}, bf16[36,432]{1,0:T(8,128)(2,1)S(1)}) custom-call(s32[1]{0:T(128)S(6)} %copy.10.len_ref, bf16[128,3456]{1,0:T(8,128)(2,1)} %bitcast.7, bf16[36,3456]{1,0:T(8,128)(2,1)S(1)} %copy-done.1, bf16[128,1152]{1,0:T(8,128)(2,1)S(1)} %bitcast.6), custom_call_target="tpu_custom_call" | custom-call | tf_op jit(solution)/shard_map/pallas_call | solution.py:654
  78.6 0.7 copy.11
  79.3 0.9 %copy.12 = bf16[1,1,128,3456]{3,2,1,0:T(8,128)(2,1)} copy(bf16[1,1,128,3456]{3,2,1,0:T(8,128)(2,1)S(1)} %bitcast.4) | data formatting | bytes 1769472
  80.2 0.6 copy.13
Async XLA Ops:
  1.3 1.0 %copy-start = (bf16[1,1,128,1152]{3,2,1,0:T(8,128)(2,1)S(1)}, bf16[1,1,128,1152]{3,2,1,0:T(8,128)(2,1)}, u32[]{:S(2)}) copy-start(bf16[1,1,128,1152]{3,2,1,0:T(8,128)(2,1)} %param.7) | copy-start | bytes 884740
  2.2 1.0 %copy-start.1 = (bf16[36,3456]{1,0:T(8,128)(2,1)S(1)}, bf16[36,3456]{1,0:T(8,128)(2,1)}, u32[]{:S(2)}) copy-start(bf16[36,3456]{1,0:T(8,128)(2,1)} %w.1) | copy-start | bytes 746500
